TPU v7x, 256 devices: a whole 4x4x8 slice. The times are simulated.
256 devices in a mesh: body: 64 (over y, z, core), across: 4 (over x).
Axes of the slice: x: 4, y: 4, z: 8, core: 2. Of those that a mesh axis runs over, the one named last changes fastest.
Arguments:
- cotangent: float32 [3, 512, 128, 256], P(None, 'body', 'across'), may hold values from -6 to 6
- shear_modulus: float32 [512, 128, 256], P('body', 'across'), may hold values from 0.3 to 3
- lame_first: float32 [512, 128, 256], P('body', 'across'), may hold values from 0.3 to 3
- inertia: float32 [512, 128, 256], P('body', 'across'), may hold values from 0.02 to 0.2
- surface_points: float32 [64, 4, 16, 3, 128], P('body', 'across'), may hold values from -0.3 to 1, as said below
- point_counts: int32 [64, 4, 16], P('body', 'across'), may hold values from 64 to 128, as said below
- surface_maps: int32 [64, 4, 16, 128], P('body', 'across'), may hold values from 0 to 65535, as said below
- contact_pairs: int32 [64, 4, 3, 256], P('body', 'across'), may hold values from 0 to 63, as said below
Outputs:
- displacement: float32 [3, 512, 128, 256], P(None, 'body', 'across')
- residual: float32 [3, 512, 128, 256], P(None, 'body', 'across')
Inputs may be any that keep to these rules, and one draw needn't show every extreme that they name: `surface_points`: coordinates 0 and 1 lie in [0, 1]; coordinate 2 lies in [0.3, 0.6] for even-numbered blocks and in [-0.3, 0] for odd-numbered blocks. `point_counts`: every device has a block with all 128 points active. `surface_maps`: the cells of one device's points are distinct. `contact_pairs`: row 0 holds even block numbers and row 2 odd block numbers below 16; row 1 is a first-split index, and the partner shares the device's second-split index. Every device names every first-split index, its own included, exactly 4 times.
All inputs are finite; a program needn't handle non-finite values.
Results may differ from a plain program's by a relative error of at most 0.0003.
Values sent between devices are 32-bit elements; how exact they have to be, the bound alone decides.
A program may use at most 192 MiB of HBM per device.

v0:
```python
import functools

import jax
import jax.numpy as jnp
from jax import lax
from jax.experimental import pallas as pl
from jax.experimental.pallas import tpu as pltpu
from jax.sharding import PartitionSpec as P

MESH = pl.DeviceIdType.MESH
CAP = 4
ROWS, COLS, DEPTH = 8, 32, 256
BLOCKS, WIDTH = 16, 128
MOVE = 3 * WIDTH
F32, BF16 = jnp.float32, jnp.bfloat16
FAR = 100.0


def iota(shape, dim):
    return lax.broadcasted_iota(jnp.int32, shape, dim)


def fiota(shape, dim):
    return iota(shape, dim).astype(F32)


def parts2(x):
    high = x.astype(BF16)
    return high, (x - high.astype(F32)).astype(BF16)


def parts3(x):
    high = x.astype(BF16).astype(F32)
    rest = x - high
    mid = rest.astype(BF16).astype(F32)
    return high, mid, rest - mid


def lanes_t(a, b):
    return lax.dot_general(a, b, (((1,), (1,)), ((), ())), preferred_element_type=F32)


def plain(a, b):
    return jnp.dot(a, b, preferred_element_type=F32)


def kernel(
    nb, na,
    c_hbm, mu_hbm, lam_hbm, inertia_hbm, pts_ref, cnt_ref, map_ref, pair_ref,
    disp_hbm, res_hbm,
    cx, qx, q2, mx, inertia, fw, ez, vh, vm, lhs, ws,
    moves0, moves1, mparts, pparts, ytab, ownc, tgtc, ownr, second, rowt, colt, forces,
    psend, pgot, msend, mgot, rsend, rgot, fsend, fgot, bsend, bgot,
    ysend, ygot, ysend1, ygot1, arsend, argot, outs,
    sem_in, sem_out, a2a_send, a2a_recv, halo_send, halo_recv, ar_send, ar_recv,
):
    b = lax.axis_index("body")
    a = lax.axis_index("across")
    slots = nb * CAP
    groups = nb // 2
    me_g = b // 2

    def wrap(i, n):
        return lax.rem(i + n, n)

    loads = [
        pltpu.make_async_copy(c_hbm, cx.at[:, pl.ds(1, ROWS)], sem_in.at[0]),
        pltpu.make_async_copy(mu_hbm, mx.at[0, pl.ds(1, ROWS)], sem_in.at[1]),
        pltpu.make_async_copy(lam_hbm, mx.at[1, pl.ds(1, ROWS)], sem_in.at[2]),
        pltpu.make_async_copy(inertia_hbm, inertia, sem_in.at[3]),
    ]
    for load in loads:
        load.start()

    table = pair_ref[...].astype(F32)
    own_row, partner_row, target_row = table[0:1], table[1:2], table[2:3]
    sub, lane = iota((slots, slots), 0), iota((slots, slots), 1)
    eye = sub == lane
    partner_col = jnp.sum(jnp.where(eye, partner_row, 0.0), axis=1, keepdims=True)
    rank = jnp.sum(
        jnp.where((partner_col == partner_row) & (sub < lane), 1.0, 0.0), axis=0, keepdims=True
    )
    slot_row = partner_row * CAP + rank
    chosen = slot_row == sub.astype(F32)
    own_col = jnp.sum(jnp.where(chosen, own_row, 0.0), axis=1, keepdims=True)
    target_col = jnp.sum(jnp.where(chosen, target_row, 0.0), axis=1, keepdims=True)
    ownc[...] = jnp.broadcast_to(own_col, (slots, WIDTH))
    tgtc[...] = jnp.broadcast_to(target_col, (slots, WIDTH))
    ownr[...] = jnp.sum(jnp.where(eye, own_col, 0.0), axis=0, keepdims=True)

    block_id = iota((BLOCKS, WIDTH), 0)
    count = jnp.zeros((BLOCKS, WIDTH), jnp.int32)
    for k in range(BLOCKS):
        count = jnp.where(block_id == k, cnt_ref[0, 0, k], count)
    active = iota((BLOCKS, WIDTH), 1) < count
    far = jnp.where(lax.rem(block_id, 2) == 0, FAR, -FAR)
    coords = [
        jnp.where(active, pts_ref[0, 0, :, 0, :] - 0.5, far),
        pts_ref[0, 0, :, 1, :] - 0.5,
        pts_ref[0, 0, :, 2, :],
    ]
    pad16 = jnp.zeros((BLOCKS, WIDTH), F32)

    def store_parts(ref, tiles):
        for c, tile in enumerate(tiles):
            stacked = jnp.concatenate([*parts3(tile)] + [pad16] * 5, axis=0)
            ref[:, c * WIDTH : (c + 1) * WIDTH] = stacked.astype(BF16)

    store_parts(pparts, coords)
    norm = coords[0] * coords[0] + coords[1] * coords[1] + coords[2] * coords[2]
    columns = [part for y in coords for part in parts3(-2.0 * y)] + [*parts3(norm)]
    for k, column in enumerate(columns):
        ytab[:, k * WIDTH : (k + 1) * WIDTH] = jnp.concatenate(
            [column] + [pad16] * 7, axis=0
        ).astype(BF16)

    lane8 = iota((8, WIDTH), 1)
    lane3 = jnp.where(lane8 < 3 * BLOCKS, lax.rem(lane8, BLOCKS), -1).astype(F32)
    lane1 = jnp.where(lane8 < BLOCKS, lane8, -1).astype(F32)
    sub8 = iota((8, WIDTH), 0)

    def select3(ids, ref):
        return plain(jnp.where(ids == lane3, 1.0, 0.0).astype(BF16), ref[...])

    def eight(ref, g):
        return jnp.concatenate([ref[2 * g], ref[2 * g + 1]], axis=0)

    def store_eight(ref, g, value):
        ref[2 * g] = value[:4]
        ref[2 * g + 1] = value[4:]

    def rows8(g):
        return pl.ds(pl.multiple_of(g * 8, 8), 8)

    def a2a(phase, src, dst, peer):
        return pltpu.make_async_remote_copy(
            src_ref=src.at[peer], dst_ref=dst.at[b],
            send_sem=a2a_send.at[phase, peer], recv_sem=a2a_recv.at[phase, b],
            device_id=(peer, a), device_id_type=MESH,
        )

    def arrival(phase, src, dst, peer):
        return pltpu.make_async_remote_copy(
            src_ref=src.at[peer], dst_ref=dst.at[peer],
            send_sem=a2a_send.at[phase, peer], recv_sem=a2a_recv.at[phase, peer],
            device_id=(peer, a), device_id_type=MESH,
        )

    def send_group(phase, src, dst, g):
        for h in range(2):
            peer = 2 * g + h

            @pl.when(peer != b)
            def _():
                a2a(phase, src, dst, peer).start()

            @pl.when(peer == b)
            def _():
                dst[peer] = src[peer]

    def wait_group(phase, src, dst, g):
        for h in range(2):
            peer = 2 * g + h

            @pl.when(peer != b)
            def _():
                arrival(phase, src, dst, peer).wait_recv()

    def each_group(body, sign):
        def step(t, carry):
            body(wrap(me_g + sign * t, groups))
            return carry

        lax.fori_loop(0, groups, step, 0)

    def points_out(g):
        at = rows8(g)
        value = jnp.concatenate([select3(ownc[at], pparts), tgtc[at]], axis=1)
        store_eight(psend, g, value)
        send_group(0, psend, pgot, g)

    each_group(points_out, 1)

    for load in loads:
        load.wait()
    up, down = wrap(b + 1, nb), wrap(b - 1, nb)
    right, left = wrap(a + 1, na), wrap(a - 1, na)

    def halo(k, src, dst, peer):
        return pltpu.make_async_remote_copy(
            src_ref=src, dst_ref=dst, send_sem=halo_send.at[k], recv_sem=halo_recv.at[k],
            device_id=peer, device_id_type=MESH,
        )

    last = ROWS
    for c in range(3):
        ysend[0, c] = cx[c, 1 : ROWS + 1, COLS - 1, :]
        ysend[1, c] = cx[c, 1 : ROWS + 1, 0, :]
    for m in range(2):
        ysend[0, 3 + m] = mx[m, 1 : ROWS + 1, COLS - 1, :]
        ysend[1, 3 + m] = mx[m, 1 : ROWS + 1, 0, :]
    halos0 = [
        halo(0, cx.at[:, last], cx.at[:, 0], (up, a)),
        halo(1, cx.at[:, 1], cx.at[:, last + 1], (down, a)),
        halo(2, mx.at[:, last], mx.at[:, 0], (up, a)),
        halo(3, mx.at[:, 1], mx.at[:, last + 1], (down, a)),
        halo(4, ysend.at[0], ygot.at[0], (b, right)),
        halo(5, ysend.at[1], ygot.at[1], (b, left)),
    ]
    for copy in halos0:
        copy.start()

    def place(k, carry):
        z = lax.rem(map_ref[0, 0, pl.ds(k, 1), :], DEPTH)
        ez[k] = jnp.where(iota((DEPTH, WIDTH), 0) == z, 1.0, 0.0).astype(BF16)
        return carry

    lax.fori_loop(0, BLOCKS, place, 0)

    def pick(vector, base, moves):
        for c in range(3):
            flat = vector[c, base : base + ROWS].reshape(ROWS * COLS, DEPTH)
            at = slice(c * 256, (c + 1) * 256)
            vh[at], vm[at] = parts2(flat)

        def step(k, rows):
            picked = plain(vh[...], ez[k]) + plain(vm[...], ez[k])
            xy = map_ref[0, 0, pl.ds(k, 1), :] // DEPTH
            mask = iota((256, WIDTH), 0) == xy
            made = []
            for c in range(3):
                kept = jnp.where(mask, picked[c * 256 : (c + 1) * 256], 0.0)
                row = jnp.sum(kept, axis=0, keepdims=True)
                made.append(jnp.where(block_id == k, row, rows[c]))
            return tuple(made)

        rows = lax.fori_loop(0, BLOCKS, step, (pad16,) * 3)
        moves[...] = jnp.concatenate(rows, axis=1)

    pick(cx, 1, moves0)

    def tiles(value):
        return [value[:, c * WIDTH : (c + 1) * WIDTH] for c in range(3)]

    def moves_out(phase, moves, src, dst):
        store_parts(mparts, tiles(moves[...]))

        def body(g):
            store_eight(src, g, select3(ownc[rows8(g)], mparts))
            send_group(phase, src, dst, g)

        each_group(body, 1)

    moves_out(1, moves0, msend, mgot)

    row32, lane256 = iota((COLS, DEPTH), 0), iota((COLS, DEPTH), 1)

    def clear_edges(xs, yhalo):
        @pl.when(b == 0)
        def _():
            for x in xs:
                x[:, 0] = jnp.zeros_like(x[:, 0])

        @pl.when(b == nb - 1)
        def _():
            for x in xs:
                x[:, last + 1] = jnp.zeros_like(x[:, last + 1])

        @pl.when(a == 0)
        def _():
            yhalo[0] = jnp.zeros_like(yhalo[0])

        @pl.when(a == na - 1)
        def _():
            yhalo[1] = jnp.zeros_like(yhalo[1])

    def beside(v, low, high):
        return (
            jnp.where(row32 == COLS - 1, high, pltpu.roll(v, COLS - 1, 0)),
            jnp.where(row32 == 0, low, pltpu.roll(v, 1, 0)),
            jnp.where(lane256 == DEPTH - 1, 0.0, pltpu.roll(v, DEPTH - 1, 1)),
            jnp.where(lane256 == 0, 0.0, pltpu.roll(v, 1, 1)),
        )

    def faces(i, carry):
        mu, lam = mx[0, i + 1], mx[1, i + 1]
        near_mu = (mx[0, i + 2], mx[0, i]) + beside(
            mu, ygot[0, 3, pl.ds(i, 1), :], ygot[1, 3, pl.ds(i, 1), :]
        )
        near_lam = (mx[1, i + 2], mx[1, i]) + beside(
            lam, ygot[0, 4, pl.ds(i, 1), :], ygot[1, 4, pl.ds(i, 1), :]
        )
        cut = nb // 4
        open_high = jnp.where((b == cut - 1) & (i == ROWS - 1), 0.0, 0.5)
        open_low = jnp.where((b == cut) & (i == 0), 0.0, 0.5)
        for k in range(6):
            half = (open_high, open_low, 0.5, 0.5, 0.5, 0.5)[k]
            plain_weight = half * (mu + near_mu[k])
            fw[k, 0, i] = plain_weight
            fw[k, 1, i] = 2.0 * plain_weight + half * (lam + near_lam[k])
        return carry

    def elastic(vector, yhalo, out, base, others):
        def plane(i, sums):
            sums = list(sums)
            for c in range(3):
                v = vector[c, i + 1]
                near = (vector[c, i + 2], vector[c, i]) + beside(
                    v, yhalo[0, c, pl.ds(i, 1), :], yhalo[1, c, pl.ds(i, 1), :]
                )
                value = inertia[i] * v
                for k in range(6):
                    value = value + fw[k, int(k // 2 == c), i] * (v - near[k])
                out[c, base + i] = value
                for n, other in enumerate(others):
                    sums[n] = sums[n] + value * other[c, i + 1]
            return tuple(sums)

        zero = jnp.zeros((COLS, DEPTH), F32)
        return lax.fori_loop(0, ROWS, plane, (zero,) * len(others))

    for copy in halos0:
        copy.wait_recv()
    clear_edges((cx, mx), ygot)
    lax.fori_loop(0, ROWS, faces, 0)
    (c_ec,) = elastic(cx, ygot, qx, 1, (cx,))
    pick(qx, 1, moves1)

    ones8 = jnp.ones((8, WIDTH), F32)

    def weigh(g):
        wait_group(0, psend, pgot, g)
        got = eight(pgot, g)
        ids = got[:, MOVE:]
        ys = plain(jnp.where(ids == lane1, 1.0, 0.0).astype(BF16), ytab[...])
        y = [ys[:, k * WIDTH : (k + 1) * WIDTH] for k in range(12)]
        xs = tiles(got)
        firsts, seconds = [], []
        for c in range(3):
            xh, xm, xl = parts3(xs[c])
            yh, ym, yl = y[3 * c : 3 * c + 3]
            firsts += [xh, xh, xm, xm, xh, xl]
            seconds += [yh, ym, yh, ym, yl, yh]
        norm = xs[0] * xs[0] + xs[1] * xs[1] + xs[2] * xs[2]
        firsts += [*parts3(norm), ones8, ones8, ones8]
        seconds += [ones8, ones8, ones8, *y[9:]]
        zero8 = jnp.zeros((8, WIDTH), F32)
        left_side = jnp.concatenate(firsts + [zero8] * 8, axis=0).T.astype(BF16)
        for r in range(8):
            right_side = jnp.concatenate(
                [jnp.where(sub8 == r, s, 0.0) for s in seconds] + [zero8] * 8, axis=0
            ).astype(BF16)
            squared = jnp.minimum(plain(left_side, right_side), 1.0)
            inverse = 1.0 / squared
            weight = 0.005 * (inverse * (inverse + 2.0) - 3.0) - 0.01 * jnp.log(squared)
            high, low = parts2(weight)
            ws[g * 8 + r, 0:WIDTH] = high
            ws[g * 8 + r, WIDTH : 2 * WIDTH] = low

    def stack(value, extra):
        rows = []
        for tile in tiles(value):
            high = tile.astype(BF16).astype(F32)
            rows += [high, tile - high]
        return jnp.concatenate(rows + extra, axis=0).astype(BF16)

    def sides(g, src, dst, first_phase):
        got = eight(dst, g)
        mine = select3(pgot_ids(g), mparts)
        extra = [ones8, ones8] if first_phase else []
        v_rows, u_rows = stack(got, extra), stack(mine, extra)
        v_rows = jnp.concatenate([v_rows, v_rows], axis=1)
        count = 4 if first_phase else 3
        into_second = [jnp.zeros((8, WIDTH), F32)] * count
        into_first = [jnp.zeros((8, WIDTH), F32)] * count
        for r in range(8):
            w = ws[g * 8 + r]
            to_second = plain(v_rows, w)
            to_first = lanes_t(u_rows, w)
            to_first = to_first[:, :WIDTH] + to_first[:, WIDTH:]
            for k in range(count):
                high, low = slice(16 * k, 16 * k + 8), slice(16 * k + 8, 16 * k + 16)
                if k < 3:
                    s, f = to_second[high] + to_second[low], to_first[high] + to_first[low]
                else:
                    s, f = to_second[high], to_first[high]
                into_second[k] = jnp.where(sub8 == r, s, into_second[k])
                into_first[k] = jnp.where(sub8 == r, f, into_first[k])
        at = rows8(g)
        if first_phase:
            rowt[at], colt[at] = into_first[3], into_second[3]
        row_total, col_total = rowt[at], colt[at]
        second[at] = jnp.concatenate(
            [u * col_total - s for u, s in zip(tiles(mine), into_second)], axis=1
        )
        return jnp.concatenate(
            [v * row_total - f for v, f in zip(tiles(got), into_first)], axis=1
        )

    def pgot_ids(g):
        return jnp.concatenate([pgot[2 * g, :, MOVE:], pgot[2 * g + 1, :, MOVE:]], axis=0)

    def group0(g):
        weigh(g)
        wait_group(1, msend, mgot, g)
        store_eight(rsend, g, sides(g, msend, mgot, True))
        send_group(2, rsend, rgot, g)

    each_group(group0, -1)

    def collect(phase, src, dst):
        each_group(lambda g: wait_group(phase, src, dst, g), -1)
        returned = jnp.concatenate([eight(dst, g) for g in range(groups)], axis=0)
        ids = jnp.concatenate([pgot_ids(g) for g in range(groups)], axis=0)
        ids_row = jnp.sum(jnp.where(eye, ids[:, 0:1], 0.0), axis=0, keepdims=True)
        block = fiota((BLOCKS, slots), 0)
        to_own = jnp.where(block == ownr[...], 1.0, 0.0).astype(BF16)
        to_target = jnp.where(block == ids_row, 1.0, 0.0).astype(BF16)
        rh, rm = parts2(returned)
        sh, sm = parts2(second[...])
        forces[...] = (plain(to_own, rh) + plain(to_own, rm)) + (
            plain(to_target, sh) + plain(to_target, sm)
        )

    def spread(out, base):
        for part in range(2):
            for k in range(BLOCKS):
                at = slice(k * WIDTH, (k + 1) * WIDTH)
                mask = iota((256, WIDTH), 0) == map_ref[0, 0, k : k + 1, :] // DEPTH
                for c in range(3):
                    force = forces[k : k + 1, c * WIDTH : (c + 1) * WIDTH]
                    high = force.astype(BF16).astype(F32)
                    kept = high if part == 0 else force - high
                    lhs[c, part, :, at] = jnp.where(mask, kept, 0.0).astype(BF16)
        cells = jnp.concatenate([ez[k] for k in range(BLOCKS)], axis=1)
        for c in range(3):
            total = lanes_t(lhs[c, 0], cells) + lanes_t(lhs[c, 1], cells)
            out[c, base : base + ROWS] = out[c, base : base + ROWS] + total.reshape(
                ROWS, COLS, DEPTH
            )

    near = min(16, nb)
    place_near, base_near = lax.rem(b, near), (b // near) * near
    far_count = (nb // near) * na
    place_far = (b // near) * na + a

    def peer_of(stage, other):
        if stage == 0:
            return (base_near + other, a)
        return ((other // na) * near + place_near, lax.rem(other, na))

    def ar_copy(n, stage, peer, slot):
        return pltpu.make_async_remote_copy(
            src_ref=arsend.at[n, stage], dst_ref=argot.at[n, stage, slot],
            send_sem=ar_send.at[n, stage, peer], recv_sem=ar_recv.at[n, stage, slot],
            device_id=peer_of(stage, peer), device_id_type=MESH,
        )

    def ar_start(n, stage, value):
        own, size = ((place_near, near), (place_far, far_count))[stage]
        arsend[n, stage] = value

        def step(t, carry):
            ar_copy(n, stage, wrap(own + t, size), own).start()
            return carry

        lax.fori_loop(1, size, step, 0)
        argot[n, stage, own] = value

    def ar_finish(n, stage):
        own, size = ((place_near, near), (place_far, far_count))[stage]

        def step(t, carry):
            other = wrap(own + t, size)
            copy = ar_copy(n, stage, other, other)
            copy.wait_recv()
            copy.wait_send()
            return carry

        lax.fori_loop(1, size, step, 0)
        total = argot[n, stage, 0]
        for k in range(1, size):
            total = total + argot[n, stage, k]
        return total

    def rows_of(*sums):
        row = iota((8, WIDTH), 0)
        value = jnp.zeros((8, WIDTH), F32)
        for k, s in enumerate(sums):
            folded = jnp.sum(s, axis=0, keepdims=True)
            folded = sum(
                folded[:, j : j + WIDTH] for j in range(0, folded.shape[1], WIDTH)
            )
            value = jnp.where(row == k, folded, value)
        return value

    def scalar(total, k):
        return jnp.sum(total[k : k + 1], axis=1, keepdims=True)

    def whole(vector, base):
        return [vector[c, base + i] for c in range(3) for i in range(ROWS)]

    collect(2, rsend, rgot)
    moves1[...] = moves1[...] + forces[...]
    moves_out(3, moves1, fsend, fgot)
    spread(qx, 1)
    for c in range(3):
        ysend1[0, c] = qx[c, 1 : ROWS + 1, COLS - 1, :]
        ysend1[1, c] = qx[c, 1 : ROWS + 1, 0, :]
    halos1 = [
        halo(6, qx.at[:, last], qx.at[:, 0], (up, a)),
        halo(7, qx.at[:, 1], qx.at[:, last + 1], (down, a)),
        halo(8, ysend1.at[0], ygot1.at[0], (b, right)),
        halo(9, ysend1.at[1], ygot1.at[1], (b, left)),
    ]
    for copy in halos1:
        copy.start()
    c_c = jnp.zeros((COLS, DEPTH), F32)
    for v in whole(cx, 1):
        c_c = c_c + v * v
    ar_start(0, 0, rows_of(c_c, c_ec, moves0[...] * forces[...]))
    for copy in halos1:
        copy.wait_recv()
    clear_edges((qx,), ygot1)
    elastic(qx, ygot1, q2, 0, ())
    ar_start(0, 1, ar_finish(0, 0))

    def group1(g):
        wait_group(3, fsend, fgot, g)
        store_eight(bsend, g, sides(g, fsend, fgot, False))
        send_group(4, bsend, bgot, g)

    each_group(group1, -1)

    total0 = ar_finish(0, 1)
    norm0 = scalar(total0, 0)
    step0 = norm0 / (scalar(total0, 1) + scalar(total0, 2))

    def products(i, sums):
        r_r, r_ar = sums
        for c in range(3):
            q = qx[c, i + 1]
            r = cx[c, i + 1] - step0 * q
            r_r = r_r + r * r
            r_ar = r_ar + r * (q - step0 * q2[c, i])
        return r_r, r_ar

    zero = jnp.zeros((COLS, DEPTH), F32)
    r_r, r_ar = lax.fori_loop(0, ROWS, products, (zero, zero))
    collect(4, bsend, bgot)
    r_moves = moves0[...] - step0 * moves1[...]
    ar_start(1, 0, rows_of(r_r, r_ar, -step0 * (r_moves * forces[...])))
    spread(q2, 0)
    ar_start(1, 1, ar_finish(1, 0))
    total1 = ar_finish(1, 1)
    norm1 = scalar(total1, 0)
    product = scalar(total1, 1) + scalar(total1, 2)
    ratio = norm1 / norm0
    step1 = norm1 / (product - ratio * norm1 / step0)
    on_first = step0 + step1 * (1.0 + ratio)
    on_second = step1 * step0

    def finish(i, carry):
        for c in range(3):
            v, q = cx[c, i + 1], qx[c, i + 1]
            outs[0, c, i] = on_first * v - on_second * q
            outs[1, c, i] = v - on_first * q + on_second * q2[c, i]
        return carry

    lax.fori_loop(0, ROWS, finish, 0)
    stores = [
        pltpu.make_async_copy(outs.at[0], disp_hbm, sem_out.at[0]),
        pltpu.make_async_copy(outs.at[1], res_hbm, sem_out.at[1]),
    ]
    for store in stores:
        store.start()
    for copy in halos0 + halos1:
        copy.wait_send()

    def drain(t, carry):
        peer = wrap(b + t, nb)
        for phase, (src, dst) in enumerate(
            ((psend, pgot), (msend, mgot), (rsend, rgot), (fsend, fgot), (bsend, bgot))
        ):
            a2a(phase, src, dst, peer).wait_send()
        return carry

    lax.fori_loop(1, nb, drain, 0)
    for store in stores:
        store.wait()


def on_device(nb, na, cotangent, shear, lame, inertia, points, counts, maps, pairs):
    slots = nb * CAP
    grid = (3, ROWS, COLS, DEPTH)
    near = min(16, nb)
    peers = max(near, (nb // near) * na)

    def buffers(width):
        return [pltpu.VMEM((nb, CAP, width), F32)] * 2

    scratch = [
        pltpu.VMEM((3, ROWS + 2, COLS, DEPTH), F32),
        pltpu.VMEM((3, ROWS + 2, COLS, DEPTH), F32),
        pltpu.VMEM(grid, F32),
        pltpu.VMEM((2, ROWS + 2, COLS, DEPTH), F32),
        pltpu.VMEM((ROWS, COLS, DEPTH), F32),
        pltpu.VMEM((6, 2, ROWS, COLS, DEPTH), F32),
        pltpu.VMEM((BLOCKS, DEPTH, WIDTH), BF16),
        pltpu.VMEM((768, DEPTH), BF16),
        pltpu.VMEM((768, DEPTH), BF16),
        pltpu.VMEM((3, 2, 256, BLOCKS * WIDTH), BF16),
        pltpu.VMEM((slots, 2 * WIDTH, WIDTH), BF16),
        pltpu.VMEM((BLOCKS, MOVE), F32),
        pltpu.VMEM((BLOCKS, MOVE), F32),
        pltpu.VMEM((WIDTH, MOVE), BF16),
        pltpu.VMEM((WIDTH, MOVE), BF16),
        pltpu.VMEM((WIDTH, 12 * WIDTH), BF16),
        pltpu.VMEM((slots, WIDTH), F32),
        pltpu.VMEM((slots, WIDTH), F32),
        pltpu.VMEM((1, slots), F32),
        pltpu.VMEM((slots, MOVE), F32),
        pltpu.VMEM((slots, WIDTH), F32),
        pltpu.VMEM((slots, WIDTH), F32),
        pltpu.VMEM((BLOCKS, MOVE), F32),
        *buffers(MOVE + WIDTH),
        *buffers(MOVE),
        *buffers(MOVE),
        *buffers(MOVE),
        *buffers(MOVE),
        pltpu.VMEM((2, 5, ROWS, DEPTH), F32),
        pltpu.VMEM((2, 5, ROWS, DEPTH), F32),
        pltpu.VMEM((2, 3, ROWS, DEPTH), F32),
        pltpu.VMEM((2, 3, ROWS, DEPTH), F32),
        pltpu.VMEM((2, 2, 8, WIDTH), F32),
        pltpu.VMEM((2, 2, peers, 8, WIDTH), F32),
        pltpu.VMEM((2,) + grid, F32),
        pltpu.SemaphoreType.DMA((4,)),
        pltpu.SemaphoreType.DMA((2,)),
        pltpu.SemaphoreType.DMA((5, nb)),
        pltpu.SemaphoreType.DMA((5, nb)),
        pltpu.SemaphoreType.DMA((10,)),
        pltpu.SemaphoreType.DMA((10,)),
        pltpu.SemaphoreType.DMA((2, 2, peers)),
        pltpu.SemaphoreType.DMA((2, 2, peers)),
    ]
    return pl.pallas_call(
        functools.partial(kernel, nb, na),
        out_shape=[jax.ShapeDtypeStruct(grid, F32)] * 2,
        in_specs=[pl.BlockSpec(memory_space=pl.ANY)] * 4
        + [
            pl.BlockSpec(memory_space=pltpu.VMEM),
            pl.BlockSpec(memory_space=pltpu.SMEM),
            pl.BlockSpec(memory_space=pltpu.VMEM),
            pl.BlockSpec(memory_space=pltpu.VMEM),
        ],
        out_specs=[pl.BlockSpec(memory_space=pl.ANY)] * 2,
        scratch_shapes=scratch,
        compiler_params=pltpu.CompilerParams(
            has_side_effects=True, vmem_limit_bytes=58 * 2**20
        ),
        name="adjoint_cg",
    )(cotangent, shear, lame, inertia, points, counts, maps, pairs[0, 0])


def solution(mesh):
    nb, na = mesh.shape["body"], mesh.shape["across"]
    split = P("body", "across")
    vector = P(None, "body", "across", None)
    return jax.shard_map(
        functools.partial(on_device, nb, na),
        mesh=mesh,
        in_specs=(vector, split, split, split, split, split, split, split),
        out_specs=(vector, vector),
        check_vma=False,
    )
```

profile of v0, /device:TPU:1, one launch (start us, length us, event | category | flops | bytes accessed | tf_op | source)
XLA Modules:
  0.0 147.0 jit_solution(17252567497980074022)
XLA Ops:
  0.6 1.3 copy.13
  1.9 1.4 copy.10.pts_ref
  3.3 140.6 %adjoint_cg.1 = (f32[3,8,32,256]{3,2,1,0:T(8,128)}, f32[3,8,32,256]{3,2,1,0:T(8,128)}) custom-call(f32[3,8,32,256]{3,2,1,0:T(8,128)} %c_hbm.1, f32[8,32,256]{2,1,0:T(8,128)} %mu_hbm.1, f32[8,32,256]{2,1,0:T(8,128)} %lam_hbm.1, f32[8,32,256]{2,1,0:T(8,128)} %inertia_hbm.1, f32[1,1,16,3,128]{4,3,2,1,0:T(4,128)} %copy.10.pts_ref, s32[1,1,16]{2,1,0:T(1,128)} %cnt_ref.1, ...), custom_call_target="tpu_custom_call" | custom-call | tf_op jit(solution)/shard_map/adjoint_cg/pallas_call | solution.py:647
  143.9 0.0 copy-start
  143.9 2.2 %copy.16 = f32[3,8,32,256]{3,2,1,0:T(8,128)} copy(f32[3,8,32,256]{3,2,1,0:T(8,128)} %get-tuple-element.4) | data formatting | bytes 1572864
  146.1 0.0 copy-done
  146.1 0.9 copy.17
Async XLA Ops:
  143.9 2.2 %copy-start = (f32[3,8,32,256]{3,2,1,0:T(8,128)S(1)}, f32[3,8,32,256]{3,2,1,0:T(8,128)}, u32[]{:S(2)}) copy-start(f32[3,8,32,256]{3,2,1,0:T(8,128)} %get-tuple-element.5) | copy-start | bytes 2359300
where the time goes:
time: 147 us
  Pallas kernels  141 us (96%)
  local copies, waits for them, and re-layouts  5.69 us (4%)
    pallas_call x1, Pallas kernels, on_device(): pl.pallas_call(functools.partial(kernel, nb, na), out_shape=[jax.ShapeDty...  141 us
    unnamed x6, local copies, waits for them, and re-layouts  5.69 us

commit v1 on v0

--- a/solution.py
+++ b/solution.py
@@ -48,8 +48,8 @@
     nb, na,
     c_hbm, mu_hbm, lam_hbm, inertia_hbm, pts_ref, cnt_ref, map_ref, pair_ref,
     disp_hbm, res_hbm,
-    cx, qx, q2, mx, inertia, fw, ez, vh, vm, lhs, ws,
-    moves0, moves1, mparts, pparts, ytab, ownc, tgtc, ownr, second, rowt, colt, forces,
+    cx, qx, q2, mx, inertia, fw, ez, vhm, lhs, ws,
+    moves0, moves1, mparts, pparts, own3, tgtc, ownr, second, rowt, colt, forces,
     psend, pgot, msend, mgot, rsend, rgot, fsend, fgot, bsend, bgot,
     ysend, ygot, ysend1, ygot1, arsend, argot, outs,
     sem_in, sem_out, a2a_send, a2a_recv, halo_send, halo_recv, ar_send, ar_recv,
@@ -58,7 +58,8 @@
     a = lax.axis_index("across")
     slots = nb * CAP
     groups = nb // 2
-    me_g = b // 2
+    chunks = nb // 4
+    me_q = b // 4
 
     def wrap(i, n):
         return lax.rem(i + n, n)
@@ -72,8 +73,7 @@
     for load in loads:
         load.start()
 
-    table = pair_ref[...].astype(F32)
-    own_row, partner_row, target_row = table[0:1], table[1:2], table[2:3]
+    own_row, partner_row, target_row = (pair_ref[k].astype(F32) for k in range(3))
     sub, lane = iota((slots, slots), 0), iota((slots, slots), 1)
     eye = sub == lane
     partner_col = jnp.sum(jnp.where(eye, partner_row, 0.0), axis=1, keepdims=True)
@@ -84,7 +84,6 @@
     chosen = slot_row == sub.astype(F32)
     own_col = jnp.sum(jnp.where(chosen, own_row, 0.0), axis=1, keepdims=True)
     target_col = jnp.sum(jnp.where(chosen, target_row, 0.0), axis=1, keepdims=True)
-    ownc[...] = jnp.broadcast_to(own_col, (slots, WIDTH))
     tgtc[...] = jnp.broadcast_to(target_col, (slots, WIDTH))
     ownr[...] = jnp.sum(jnp.where(eye, own_col, 0.0), axis=0, keepdims=True)
 
@@ -95,9 +94,9 @@
     active = iota((BLOCKS, WIDTH), 1) < count
     far = jnp.where(lax.rem(block_id, 2) == 0, FAR, -FAR)
     coords = [
-        jnp.where(active, pts_ref[0, 0, :, 0, :] - 0.5, far),
-        pts_ref[0, 0, :, 1, :] - 0.5,
-        pts_ref[0, 0, :, 2, :],
+        jnp.where(active, pts_ref[0] - 0.5, far),
+        pts_ref[1] - 0.5,
+        pts_ref[2],
     ]
     pad16 = jnp.zeros((BLOCKS, WIDTH), F32)
 
@@ -107,17 +106,13 @@
             ref[:, c * WIDTH : (c + 1) * WIDTH] = stacked.astype(BF16)
 
     store_parts(pparts, coords)
-    norm = coords[0] * coords[0] + coords[1] * coords[1] + coords[2] * coords[2]
-    columns = [part for y in coords for part in parts3(-2.0 * y)] + [*parts3(norm)]
-    for k, column in enumerate(columns):
-        ytab[:, k * WIDTH : (k + 1) * WIDTH] = jnp.concatenate(
-            [column] + [pad16] * 7, axis=0
-        ).astype(BF16)
-
     lane8 = iota((8, WIDTH), 1)
     lane3 = jnp.where(lane8 < 3 * BLOCKS, lax.rem(lane8, BLOCKS), -1).astype(F32)
-    lane1 = jnp.where(lane8 < BLOCKS, lane8, -1).astype(F32)
     sub8 = iota((8, WIDTH), 0)
+
+    lanes = iota((slots, WIDTH), 1)
+    lanes3 = jnp.where(lanes < 3 * BLOCKS, lax.rem(lanes, BLOCKS), -1).astype(F32)
+    own3[...] = jnp.where(own_col == lanes3, 1.0, 0.0).astype(BF16)
 
     def select3(ids, ref):
         return plain(jnp.where(ids == lane3, 1.0, 0.0).astype(BF16), ref[...])
@@ -135,20 +130,24 @@
     def a2a(phase, src, dst, peer):
         return pltpu.make_async_remote_copy(
             src_ref=src.at[peer], dst_ref=dst.at[b],
-            send_sem=a2a_send.at[phase, peer], recv_sem=a2a_recv.at[phase, b],
+            send_sem=a2a_send.at[phase], recv_sem=a2a_recv.at[phase, arrives(phase, me_q)],
             device_id=(peer, a), device_id_type=MESH,
         )
 
-    def arrival(phase, src, dst, peer):
+    def arrives(phase, q):
+        return 0 if phase in (2, 4) else q
+
+    def batch(phase, src, dst, q, first, count):
+        at = pl.ds(first, count)
         return pltpu.make_async_remote_copy(
-            src_ref=src.at[peer], dst_ref=dst.at[peer],
-            send_sem=a2a_send.at[phase, peer], recv_sem=a2a_recv.at[phase, peer],
-            device_id=(peer, a), device_id_type=MESH,
-        )
-
-    def send_group(phase, src, dst, g):
-        for h in range(2):
-            peer = 2 * g + h
+            src_ref=src.at[at], dst_ref=dst.at[at],
+            send_sem=a2a_send.at[phase], recv_sem=a2a_recv.at[phase, arrives(phase, q)],
+            device_id=(wrap(b + 1, nb), a), device_id_type=MESH,
+        )
+
+    def send_chunk(phase, src, dst, q):
+        for h in range(4):
+            peer = 4 * q + h
 
             @pl.when(peer != b)
             def _():
@@ -158,29 +157,28 @@
             def _():
                 dst[peer] = src[peer]
 
-    def wait_group(phase, src, dst, g):
-        for h in range(2):
-            peer = 2 * g + h
-
-            @pl.when(peer != b)
-            def _():
-                arrival(phase, src, dst, peer).wait_recv()
-
-    def each_group(body, sign):
+    def wait_chunk(phase, src, dst, q):
+        @pl.when(q != me_q)
+        def _():
+            batch(phase, src, dst, q, 4 * q, 4).wait_recv()
+
+        @pl.when(q == me_q)
+        def _():
+            batch(phase, src, dst, q, 4 * q, 3).wait_recv()
+
+    def each_chunk(body, sign):
         def step(t, carry):
-            body(wrap(me_g + sign * t, groups))
+            body(wrap(me_q + sign * t, chunks))
             return carry
 
-        lax.fori_loop(0, groups, step, 0)
-
-    def points_out(g):
-        at = rows8(g)
-        value = jnp.concatenate([select3(ownc[at], pparts), tgtc[at]], axis=1)
-        store_eight(psend, g, value)
-        send_group(0, psend, pgot, g)
-
-    each_group(points_out, 1)
-
+        lax.fori_loop(0, chunks, step, 0)
+
+    def store_all(ref, value):
+        for k in range(nb):
+            ref[k] = value[k * CAP : (k + 1) * CAP]
+
+    store_all(psend, jnp.concatenate([plain(own3[...], pparts[...]), tgtc[...]], axis=1))
+    each_chunk(lambda q: send_chunk(0, psend, pgot, q), 1)
     for load in loads:
         load.wait()
     up, down = wrap(b + 1, nb), wrap(b - 1, nb)
@@ -210,31 +208,35 @@
     for copy in halos0:
         copy.start()
 
+    def map_row(k):
+        pair = map_ref[0, 0, pl.ds(2 * k, 1), :], map_ref[0, 0, pl.ds(2 * k + 1, 1), :]
+        return jnp.concatenate(pair, axis=1)
+
     def place(k, carry):
-        z = lax.rem(map_ref[0, 0, pl.ds(k, 1), :], DEPTH)
-        ez[k] = jnp.where(iota((DEPTH, WIDTH), 0) == z, 1.0, 0.0).astype(BF16)
+        z = lax.rem(map_row(k), DEPTH)
+        ez[k] = jnp.where(iota((DEPTH, 2 * WIDTH), 0) == z, 1.0, 0.0).astype(BF16)
         return carry
 
-    lax.fori_loop(0, BLOCKS, place, 0)
+    lax.fori_loop(0, BLOCKS // 2, place, 0)
 
     def pick(vector, base, moves):
         for c in range(3):
             flat = vector[c, base : base + ROWS].reshape(ROWS * COLS, DEPTH)
             at = slice(c * 256, (c + 1) * 256)
-            vh[at], vm[at] = parts2(flat)
+            vhm[at, :DEPTH], vhm[at, DEPTH:] = parts2(flat)
 
         def step(k, rows):
-            picked = plain(vh[...], ez[k]) + plain(vm[...], ez[k])
-            xy = map_ref[0, 0, pl.ds(k, 1), :] // DEPTH
-            mask = iota((256, WIDTH), 0) == xy
+            picked = plain(vhm[...], jnp.concatenate([ez[k], ez[k]], axis=0))
+            mask = iota((256, 2 * WIDTH), 0) == map_row(k) // DEPTH
             made = []
             for c in range(3):
                 kept = jnp.where(mask, picked[c * 256 : (c + 1) * 256], 0.0)
                 row = jnp.sum(kept, axis=0, keepdims=True)
-                made.append(jnp.where(block_id == k, row, rows[c]))
+                lower = jnp.where(block_id == 2 * k, row[:, :WIDTH], rows[c])
+                made.append(jnp.where(block_id == 2 * k + 1, row[:, WIDTH:], lower))
             return tuple(made)
 
-        rows = lax.fori_loop(0, BLOCKS, step, (pad16,) * 3)
+        rows = lax.fori_loop(0, BLOCKS // 2, step, (pad16,) * 3)
         moves[...] = jnp.concatenate(rows, axis=1)
 
     pick(cx, 1, moves0)
@@ -245,11 +247,8 @@
     def moves_out(phase, moves, src, dst):
         store_parts(mparts, tiles(moves[...]))
 
-        def body(g):
-            store_eight(src, g, select3(ownc[rows8(g)], mparts))
-            send_group(phase, src, dst, g)
-
-        each_group(body, 1)
+        store_all(src, plain(own3[...], mparts[...]))
+        each_chunk(lambda q: send_chunk(phase, src, dst, q), 1)
 
     moves_out(1, moves0, msend, mgot)
 
@@ -329,87 +328,87 @@
     ones8 = jnp.ones((8, WIDTH), F32)
 
     def weigh(g):
-        wait_group(0, psend, pgot, g)
         got = eight(pgot, g)
         ids = got[:, MOVE:]
-        ys = plain(jnp.where(ids == lane1, 1.0, 0.0).astype(BF16), ytab[...])
-        y = [ys[:, k * WIDTH : (k + 1) * WIDTH] for k in range(12)]
-        xs = tiles(got)
-        firsts, seconds = [], []
-        for c in range(3):
-            xh, xm, xl = parts3(xs[c])
-            yh, ym, yl = y[3 * c : 3 * c + 3]
-            firsts += [xh, xh, xm, xm, xh, xl]
-            seconds += [yh, ym, yh, ym, yl, yh]
-        norm = xs[0] * xs[0] + xs[1] * xs[1] + xs[2] * xs[2]
-        firsts += [*parts3(norm), ones8, ones8, ones8]
-        seconds += [ones8, ones8, ones8, *y[9:]]
-        zero8 = jnp.zeros((8, WIDTH), F32)
-        left_side = jnp.concatenate(firsts + [zero8] * 8, axis=0).T.astype(BF16)
+        ys = tiles(select3(ids, pparts))
+        pad = jnp.zeros((WIDTH - 24, WIDTH), F32)
+        xs = jnp.concatenate(tiles(got) + [pad], axis=0).T
         for r in range(8):
-            right_side = jnp.concatenate(
-                [jnp.where(sub8 == r, s, 0.0) for s in seconds] + [zero8] * 8, axis=0
-            ).astype(BF16)
-            squared = jnp.minimum(plain(left_side, right_side), 1.0)
+            squared = None
+            for c in range(3):
+                apart = xs[:, 8 * c + r : 8 * c + r + 1] - ys[c][r : r + 1]
+                squared = apart * apart if squared is None else squared + apart * apart
+            squared = jnp.minimum(squared, 1.0)
             inverse = 1.0 / squared
             weight = 0.005 * (inverse * (inverse + 2.0) - 3.0) - 0.01 * jnp.log(squared)
             high, low = parts2(weight)
             ws[g * 8 + r, 0:WIDTH] = high
             ws[g * 8 + r, WIDTH : 2 * WIDTH] = low
 
-    def stack(value, extra):
+    def halves(value, extra):
         rows = []
         for tile in tiles(value):
             high = tile.astype(BF16).astype(F32)
             rows += [high, tile - high]
-        return jnp.concatenate(rows + extra, axis=0).astype(BF16)
-
-    def sides(g, src, dst, first_phase):
+        return rows + extra
+
+    def only(rows, keep):
+        kept = [jnp.where(keep, row, 0.0) for row in rows]
+        return jnp.concatenate(kept, axis=0).astype(BF16)
+
+    def sides(g, dst, mine, first_phase):
         got = eight(dst, g)
-        mine = select3(pgot_ids(g), mparts)
         extra = [ones8, ones8] if first_phase else []
-        v_rows, u_rows = stack(got, extra), stack(mine, extra)
-        v_rows = jnp.concatenate([v_rows, v_rows], axis=1)
-        count = 4 if first_phase else 3
-        into_second = [jnp.zeros((8, WIDTH), F32)] * count
-        into_first = [jnp.zeros((8, WIDTH), F32)] * count
-        for r in range(8):
-            w = ws[g * 8 + r]
-            to_second = plain(v_rows, w)
-            to_first = lanes_t(u_rows, w)
-            to_first = to_first[:, :WIDTH] + to_first[:, WIDTH:]
-            for k in range(count):
-                high, low = slice(16 * k, 16 * k + 8), slice(16 * k + 8, 16 * k + 16)
-                if k < 3:
-                    s, f = to_second[high] + to_second[low], to_first[high] + to_first[low]
-                else:
-                    s, f = to_second[high], to_first[high]
-                into_second[k] = jnp.where(sub8 == r, s, into_second[k])
-                into_first[k] = jnp.where(sub8 == r, f, into_first[k])
+        v_rows, u_rows = halves(got, extra), halves(mine, extra)
+        w = [ws[g * 8 + r] for r in range(8)]
+        v_side, w_side = [], []
+        for q in range(4):
+            kept = only(v_rows, lax.rem(sub8, 4) == q)
+            v_side += [kept, kept]
+            w_side.append(jnp.concatenate([w[q], w[q + 4]], axis=1))
+        to_second = plain(jnp.concatenate(v_side, axis=1), jnp.concatenate(w_side, axis=0))
+        u_side = jnp.concatenate([only(u_rows, sub8 == r) for r in range(8)], axis=1)
+        to_first = lanes_t(u_side, jnp.concatenate(w, axis=1))
+        to_first = to_first[:, :WIDTH] + to_first[:, WIDTH:]
+        into_second, into_first = [], []
+        for k in range(len(v_rows)):
+            at = slice(8 * k, 8 * k + 8)
+            into_second.append(
+                jnp.where(sub8 < 4, to_second[at, :WIDTH], to_second[at, WIDTH:])
+            )
+            into_first.append(to_first[at])
         at = rows8(g)
         if first_phase:
-            rowt[at], colt[at] = into_first[3], into_second[3]
+            rowt[at], colt[at] = into_first[6], into_second[6]
         row_total, col_total = rowt[at], colt[at]
+
+        def force(move, total, parts, c):
+            return move * total - (parts[2 * c] + parts[2 * c + 1])
+
         second[at] = jnp.concatenate(
-            [u * col_total - s for u, s in zip(tiles(mine), into_second)], axis=1
+            [force(u, col_total, into_second, c) for c, u in enumerate(tiles(mine))], axis=1
         )
         return jnp.concatenate(
-            [v * row_total - f for v, f in zip(tiles(got), into_first)], axis=1
+            [force(v, row_total, into_first, c) for c, v in enumerate(tiles(got))], axis=1
         )
 
     def pgot_ids(g):
         return jnp.concatenate([pgot[2 * g, :, MOVE:], pgot[2 * g + 1, :, MOVE:]], axis=0)
 
-    def group0(g):
-        weigh(g)
-        wait_group(1, msend, mgot, g)
-        store_eight(rsend, g, sides(g, msend, mgot, True))
-        send_group(2, rsend, rgot, g)
-
-    each_group(group0, -1)
+    def chunk0(q):
+        wait_chunk(0, psend, pgot, q)
+        for g in (2 * q, 2 * q + 1):
+            weigh(g)
+        wait_chunk(1, msend, mgot, q)
+        for g in (2 * q, 2 * q + 1):
+            mine = select3(pgot_ids(g), mparts)
+            store_eight(rsend, g, sides(g, mgot, mine, True))
+        send_chunk(2, rsend, rgot, q)
+
+    each_chunk(chunk0, -1)
 
     def collect(phase, src, dst):
-        each_group(lambda g: wait_group(phase, src, dst, g), -1)
+        batch(phase, src, dst, 0, 0, nb - 1).wait_recv()
         returned = jnp.concatenate([eight(dst, g) for g in range(groups)], axis=0)
         ids = jnp.concatenate([pgot_ids(g) for g in range(groups)], axis=0)
         ids_row = jnp.sum(jnp.where(eye, ids[:, 0:1], 0.0), axis=0, keepdims=True)
@@ -432,7 +431,7 @@
                     high = force.astype(BF16).astype(F32)
                     kept = high if part == 0 else force - high
                     lhs[c, part, :, at] = jnp.where(mask, kept, 0.0).astype(BF16)
-        cells = jnp.concatenate([ez[k] for k in range(BLOCKS)], axis=1)
+        cells = jnp.concatenate([ez[k] for k in range(BLOCKS // 2)], axis=1)
         for c in range(3):
             total = lanes_t(lhs[c, 0], cells) + lanes_t(lhs[c, 1], cells)
             out[c, base : base + ROWS] = out[c, base : base + ROWS] + total.reshape(
@@ -452,7 +451,7 @@
     def ar_copy(n, stage, peer, slot):
         return pltpu.make_async_remote_copy(
             src_ref=arsend.at[n, stage], dst_ref=argot.at[n, stage, slot],
-            send_sem=ar_send.at[n, stage, peer], recv_sem=ar_recv.at[n, stage, slot],
+            send_sem=ar_send.at[n, stage], recv_sem=ar_recv.at[n, stage],
             device_id=peer_of(stage, peer), device_id_type=MESH,
         )
 
@@ -470,14 +469,14 @@
     def ar_finish(n, stage):
         own, size = ((place_near, near), (place_far, far_count))[stage]
 
-        def step(t, carry):
-            other = wrap(own + t, size)
-            copy = ar_copy(n, stage, other, other)
-            copy.wait_recv()
-            copy.wait_send()
-            return carry
-
-        lax.fori_loop(1, size, step, 0)
+        for k in range(2):
+            at = pl.ds(0, size - 1)
+            arrived = pltpu.make_async_remote_copy(
+                src_ref=argot.at[n, stage, at], dst_ref=argot.at[n, stage, at],
+                send_sem=ar_send.at[n, stage], recv_sem=ar_recv.at[n, stage],
+                device_id=peer_of(stage, wrap(own + 1, size)), device_id_type=MESH,
+            )
+            (arrived.wait_recv, arrived.wait_send)[k]()
         total = argot[n, stage, 0]
         for k in range(1, size):
             total = total + argot[n, stage, k]
@@ -525,12 +524,14 @@
     elastic(qx, ygot1, q2, 0, ())
     ar_start(0, 1, ar_finish(0, 0))
 
-    def group1(g):
-        wait_group(3, fsend, fgot, g)
-        store_eight(bsend, g, sides(g, fsend, fgot, False))
-        send_group(4, bsend, bgot, g)
-
-    each_group(group1, -1)
+    def chunk1(q):
+        wait_chunk(3, fsend, fgot, q)
+        for g in (2 * q, 2 * q + 1):
+            mine = select3(pgot_ids(g), mparts)
+            store_eight(bsend, g, sides(g, fgot, mine, False))
+        send_chunk(4, bsend, bgot, q)
+
+    each_chunk(chunk1, -1)
 
     total0 = ar_finish(0, 1)
     norm0 = scalar(total0, 0)
@@ -577,15 +578,10 @@
     for copy in halos0 + halos1:
         copy.wait_send()
 
-    def drain(t, carry):
-        peer = wrap(b + t, nb)
-        for phase, (src, dst) in enumerate(
-            ((psend, pgot), (msend, mgot), (rsend, rgot), (fsend, fgot), (bsend, bgot))
-        ):
-            a2a(phase, src, dst, peer).wait_send()
-        return carry
-
-    lax.fori_loop(1, nb, drain, 0)
+    for phase, (src, dst) in enumerate(
+        ((psend, pgot), (msend, mgot), (rsend, rgot), (fsend, fgot), (bsend, bgot))
+    ):
+        batch(phase, src, dst, 0, 0, nb - 1).wait_send()
     for store in stores:
         store.wait()
 
@@ -606,17 +602,15 @@
         pltpu.VMEM((2, ROWS + 2, COLS, DEPTH), F32),
         pltpu.VMEM((ROWS, COLS, DEPTH), F32),
         pltpu.VMEM((6, 2, ROWS, COLS, DEPTH), F32),
-        pltpu.VMEM((BLOCKS, DEPTH, WIDTH), BF16),
-        pltpu.VMEM((768, DEPTH), BF16),
-        pltpu.VMEM((768, DEPTH), BF16),
+        pltpu.VMEM((BLOCKS // 2, DEPTH, 2 * WIDTH), BF16),
+        pltpu.VMEM((768, 2 * DEPTH), BF16),
         pltpu.VMEM((3, 2, 256, BLOCKS * WIDTH), BF16),
         pltpu.VMEM((slots, 2 * WIDTH, WIDTH), BF16),
         pltpu.VMEM((BLOCKS, MOVE), F32),
         pltpu.VMEM((BLOCKS, MOVE), F32),
         pltpu.VMEM((WIDTH, MOVE), BF16),
         pltpu.VMEM((WIDTH, MOVE), BF16),
-        pltpu.VMEM((WIDTH, 12 * WIDTH), BF16),
-        pltpu.VMEM((slots, WIDTH), F32),
+        pltpu.VMEM((slots, WIDTH), BF16),
         pltpu.VMEM((slots, WIDTH), F32),
         pltpu.VMEM((1, slots), F32),
         pltpu.VMEM((slots, MOVE), F32),
@@ -637,12 +631,12 @@
         pltpu.VMEM((2,) + grid, F32),
         pltpu.SemaphoreType.DMA((4,)),
         pltpu.SemaphoreType.DMA((2,)),
-        pltpu.SemaphoreType.DMA((5, nb)),
-        pltpu.SemaphoreType.DMA((5, nb)),
+        pltpu.SemaphoreType.DMA((5,)),
+        pltpu.SemaphoreType.DMA((5, nb // 4)),
         pltpu.SemaphoreType.DMA((10,)),
         pltpu.SemaphoreType.DMA((10,)),
-        pltpu.SemaphoreType.DMA((2, 2, peers)),
-        pltpu.SemaphoreType.DMA((2, 2, peers)),
+        pltpu.SemaphoreType.DMA((2, 2)),
+        pltpu.SemaphoreType.DMA((2, 2)),
     ]
     return pl.pallas_call(
         functools.partial(kernel, nb, na),
@@ -660,7 +654,10 @@
             has_side_effects=True, vmem_limit_bytes=58 * 2**20
         ),
         name="adjoint_cg",
-    )(cotangent, shear, lame, inertia, points, counts, maps, pairs[0, 0])
+    )(
+        cotangent, shear, lame, inertia,
+        points[0, 0].transpose(1, 0, 2), counts, maps, pairs[0].transpose(1, 0, 2),
+    )
 
 
 def solution(mesh):

time: 147 us -> 128 us (0.87)
  Pallas kernels: 141 us -> 124 us
  local copies, waits for them, and re-layouts: 5.69 us -> 3.04 us
    pallas_call x1, Pallas kernels: 141 us -> 124 us  [on_device(): pl.pallas_call(functools.partial(kernel, nb, na), out_shape=[jax.ShapeDty...]
    unnamed x6 -> x4, local copies, waits for them, and re-layouts: 5.69 us -> 3.04 us
where the time goes in v1:
time: 128 us
  Pallas kernels  124 us (97%)
  local copies, waits for them, and re-layouts  3.04 us (2%)
    pallas_call x1, Pallas kernels, on_device(): pl.pallas_call(functools.partial(kernel, nb, na), out_shape=[jax.ShapeDty...  124 us
    unnamed x4, local copies, waits for them, and re-layouts  3.04 us

profile of v1, /device:TPU:1, one launch (start us, length us, event | category | flops | bytes accessed | tf_op | source)
XLA Modules:
  0.0 127.5 jit_solution(1904554827885001113)
XLA Ops:
  0.6 123.8 %adjoint_cg.1 = (f32[3,8,32,256]{3,2,1,0:T(8,128)}, f32[3,8,32,256]{3,2,1,0:T(8,128)}) custom-call(f32[3,8,32,256]{3,2,1,0:T(8,128)} %c_hbm.1, f32[8,32,256]{2,1,0:T(8,128)} %mu_hbm.1, f32[8,32,256]{2,1,0:T(8,128)} %lam_hbm.1, f32[8,32,256]{2,1,0:T(8,128)} %inertia_hbm.1, f32[3,16,128]{2,1,0:T(8,128)} %bitcast.4, s32[1,1,16]{2,1,0:T(1,128)} %cnt_ref.1, ...), custom_call_target="tpu_custom_call" | custom-call | tf_op jit(solution)/shard_map/adjoint_cg/pallas_call | solution.py:641
  124.4 0.0 copy-start
  124.5 2.2 %copy.12 = f32[3,8,32,256]{3,2,1,0:T(8,128)} copy(f32[3,8,32,256]{3,2,1,0:T(8,128)} %get-tuple-element.4) | data formatting | bytes 1572864
  126.6 0.0 copy-done
  126.6 0.9 copy.13
Async XLA Ops:
  124.4 2.2 %copy-start = (f32[3,8,32,256]{3,2,1,0:T(8,128)S(1)}, f32[3,8,32,256]{3,2,1,0:T(8,128)}, u32[]{:S(2)}) copy-start(f32[3,8,32,256]{3,2,1,0:T(8,128)} %get-tuple-element.5) | copy-start | bytes 2359300

commit v2 on v1

--- a/solution.py
+++ b/solution.py
@@ -47,11 +47,11 @@
 def kernel(
     nb, na,
     c_hbm, mu_hbm, lam_hbm, inertia_hbm, pts_ref, cnt_ref, map_ref, pair_ref,
-    disp_hbm, res_hbm,
+    q1_hbm, q2_hbm, coef_ref,
     cx, qx, q2, mx, inertia, fw, ez, vhm, lhs, ws,
     moves0, moves1, mparts, pparts, own3, tgtc, ownr, second, rowt, colt, forces,
     psend, pgot, msend, mgot, rsend, rgot, fsend, fgot, bsend, bgot,
-    ysend, ygot, ysend1, ygot1, arsend, argot, outs,
+    ysend, ygot, ysend1, ygot1, arsend, argot,
     sem_in, sem_out, a2a_send, a2a_recv, halo_send, halo_recv, ar_send, ar_recv,
 ):
     b = lax.axis_index("body")
@@ -63,6 +63,22 @@
 
     def wrap(i, n):
         return lax.rem(i + n, n)
+
+    near = min(16, nb)
+    place_near, base_near = lax.rem(b, near), (b // near) * near
+    barrier = pltpu.get_barrier_semaphore()
+
+    def greet(peer):
+        pl.semaphore_signal(barrier, inc=1, device_id=peer, device_id_type=MESH)
+
+    def greet_body(t, carry):
+        greet((wrap(b + t, nb), a))
+        return carry
+
+    lax.fori_loop(1, nb, greet_body, 0)
+    for t in range(1, na):
+        for k in range(nb // near):
+            greet((k * near + place_near, wrap(a + t, na)))
 
     loads = [
         pltpu.make_async_copy(c_hbm, cx.at[:, pl.ds(1, ROWS)], sem_in.at[0]),
@@ -166,18 +182,30 @@
         def _():
             batch(phase, src, dst, q, 4 * q, 3).wait_recv()
 
-    def each_chunk(body, sign):
+    def each_chunk(body, sign, start=0, stop=nb // 4):
         def step(t, carry):
             body(wrap(me_q + sign * t, chunks))
             return carry
 
-        lax.fori_loop(0, chunks, step, 0)
+        lax.fori_loop(start, stop, step, 0)
 
     def store_all(ref, value):
         for k in range(nb):
             ref[k] = value[k * CAP : (k + 1) * CAP]
 
     store_all(psend, jnp.concatenate([plain(own3[...], pparts[...]), tgtc[...]], axis=1))
+    def map_row(k):
+        pair = map_ref[0, 0, pl.ds(2 * k, 1), :], map_ref[0, 0, pl.ds(2 * k + 1, 1), :]
+        return jnp.concatenate(pair, axis=1)
+
+    def place(k, carry):
+        z = lax.rem(map_row(k), DEPTH)
+        ez[k] = jnp.where(iota((DEPTH, 2 * WIDTH), 0) == z, 1.0, 0.0).astype(BF16)
+        return carry
+
+    lax.fori_loop(0, BLOCKS // 2, place, 0)
+
+    pl.semaphore_wait(barrier, nb - 1 + (na - 1) * (nb // near))
     each_chunk(lambda q: send_chunk(0, psend, pgot, q), 1)
     for load in loads:
         load.wait()
@@ -208,17 +236,6 @@
     for copy in halos0:
         copy.start()
 
-    def map_row(k):
-        pair = map_ref[0, 0, pl.ds(2 * k, 1), :], map_ref[0, 0, pl.ds(2 * k + 1, 1), :]
-        return jnp.concatenate(pair, axis=1)
-
-    def place(k, carry):
-        z = lax.rem(map_row(k), DEPTH)
-        ez[k] = jnp.where(iota((DEPTH, 2 * WIDTH), 0) == z, 1.0, 0.0).astype(BF16)
-        return carry
-
-    lax.fori_loop(0, BLOCKS // 2, place, 0)
-
     def pick(vector, base, moves):
         for c in range(3):
             flat = vector[c, base : base + ROWS].reshape(ROWS * COLS, DEPTH)
@@ -317,13 +334,6 @@
 
         zero = jnp.zeros((COLS, DEPTH), F32)
         return lax.fori_loop(0, ROWS, plane, (zero,) * len(others))
-
-    for copy in halos0:
-        copy.wait_recv()
-    clear_edges((cx, mx), ygot)
-    lax.fori_loop(0, ROWS, faces, 0)
-    (c_ec,) = elastic(cx, ygot, qx, 1, (cx,))
-    pick(qx, 1, moves1)
 
     ones8 = jnp.ones((8, WIDTH), F32)
 
@@ -407,6 +417,18 @@
 
     each_chunk(chunk0, -1)
 
+    for copy in halos0:
+        copy.wait_recv()
+    clear_edges((cx, mx), ygot)
+    lax.fori_loop(0, ROWS, faces, 0)
+    (c_ec,) = elastic(cx, ygot, qx, 1, (cx,))
+    pick(qx, 1, moves1)
+    c_c = jnp.zeros((COLS, DEPTH), F32)
+    for c in range(3):
+        for i in range(ROWS):
+            c_c = c_c + cx[c, i + 1] * cx[c, i + 1]
+
+
     def collect(phase, src, dst):
         batch(phase, src, dst, 0, 0, nb - 1).wait_recv()
         returned = jnp.concatenate([eight(dst, g) for g in range(groups)], axis=0)
@@ -438,8 +460,6 @@
                 ROWS, COLS, DEPTH
             )
 
-    near = min(16, nb)
-    place_near, base_near = lax.rem(b, near), (b // near) * near
     far_count = (nb // near) * na
     place_far = (b // near) * na + a
 
@@ -495,9 +515,6 @@
 
     def scalar(total, k):
         return jnp.sum(total[k : k + 1], axis=1, keepdims=True)
-
-    def whole(vector, base):
-        return [vector[c, base + i] for c in range(3) for i in range(ROWS)]
 
     collect(2, rsend, rgot)
     moves1[...] = moves1[...] + forces[...]
@@ -514,16 +531,7 @@
     ]
     for copy in halos1:
         copy.start()
-    c_c = jnp.zeros((COLS, DEPTH), F32)
-    for v in whole(cx, 1):
-        c_c = c_c + v * v
     ar_start(0, 0, rows_of(c_c, c_ec, moves0[...] * forces[...]))
-    for copy in halos1:
-        copy.wait_recv()
-    clear_edges((qx,), ygot1)
-    elastic(qx, ygot1, q2, 0, ())
-    ar_start(0, 1, ar_finish(0, 0))
-
     def chunk1(q):
         wait_chunk(3, fsend, fgot, q)
         for g in (2 * q, 2 * q + 1):
@@ -531,7 +539,16 @@
             store_eight(bsend, g, sides(g, fgot, mine, False))
         send_chunk(4, bsend, bgot, q)
 
-    each_chunk(chunk1, -1)
+    q1_store = pltpu.make_async_copy(qx.at[:, pl.ds(1, ROWS)], q1_hbm, sem_out.at[0])
+    q1_store.start()
+    each_chunk(chunk1, -1, 0, chunks // 2)
+    ar_start(0, 1, ar_finish(0, 0))
+    each_chunk(chunk1, -1, chunks // 2, chunks)
+    for copy in halos1:
+        copy.wait_recv()
+    clear_edges((qx,), ygot1)
+    elastic(qx, ygot1, q2, 0, ())
+
 
     total0 = ar_finish(0, 1)
     norm0 = scalar(total0, 0)
@@ -552,6 +569,8 @@
     r_moves = moves0[...] - step0 * moves1[...]
     ar_start(1, 0, rows_of(r_r, r_ar, -step0 * (r_moves * forces[...])))
     spread(q2, 0)
+    q2_store = pltpu.make_async_copy(q2, q2_hbm, sem_out.at[1])
+    q2_store.start()
     ar_start(1, 1, ar_finish(1, 0))
     total1 = ar_finish(1, 1)
     norm1 = scalar(total1, 0)
@@ -561,20 +580,8 @@
     on_first = step0 + step1 * (1.0 + ratio)
     on_second = step1 * step0
 
-    def finish(i, carry):
-        for c in range(3):
-            v, q = cx[c, i + 1], qx[c, i + 1]
-            outs[0, c, i] = on_first * v - on_second * q
-            outs[1, c, i] = v - on_first * q + on_second * q2[c, i]
-        return carry
-
-    lax.fori_loop(0, ROWS, finish, 0)
-    stores = [
-        pltpu.make_async_copy(outs.at[0], disp_hbm, sem_out.at[0]),
-        pltpu.make_async_copy(outs.at[1], res_hbm, sem_out.at[1]),
-    ]
-    for store in stores:
-        store.start()
+    row = iota((8, WIDTH), 0)
+    coef_ref[...] = jnp.where(row == 0, on_first, on_second)
     for copy in halos0 + halos1:
         copy.wait_send()
 
@@ -582,8 +589,8 @@
         ((psend, pgot), (msend, mgot), (rsend, rgot), (fsend, fgot), (bsend, bgot))
     ):
         batch(phase, src, dst, 0, 0, nb - 1).wait_send()
-    for store in stores:
-        store.wait()
+    q1_store.wait()
+    q2_store.wait()
 
 
 def on_device(nb, na, cotangent, shear, lame, inertia, points, counts, maps, pairs):
@@ -628,7 +635,6 @@
         pltpu.VMEM((2, 3, ROWS, DEPTH), F32),
         pltpu.VMEM((2, 2, 8, WIDTH), F32),
         pltpu.VMEM((2, 2, peers, 8, WIDTH), F32),
-        pltpu.VMEM((2,) + grid, F32),
         pltpu.SemaphoreType.DMA((4,)),
         pltpu.SemaphoreType.DMA((2,)),
         pltpu.SemaphoreType.DMA((5,)),
@@ -638,9 +644,10 @@
         pltpu.SemaphoreType.DMA((2, 2)),
         pltpu.SemaphoreType.DMA((2, 2)),
     ]
-    return pl.pallas_call(
+    q1, q2, coef = pl.pallas_call(
         functools.partial(kernel, nb, na),
-        out_shape=[jax.ShapeDtypeStruct(grid, F32)] * 2,
+        out_shape=[jax.ShapeDtypeStruct(grid, F32)] * 2
+        + [jax.ShapeDtypeStruct((8, WIDTH), F32)],
         in_specs=[pl.BlockSpec(memory_space=pl.ANY)] * 4
         + [
             pl.BlockSpec(memory_space=pltpu.VMEM),
@@ -648,16 +655,20 @@
             pl.BlockSpec(memory_space=pltpu.VMEM),
             pl.BlockSpec(memory_space=pltpu.VMEM),
         ],
-        out_specs=[pl.BlockSpec(memory_space=pl.ANY)] * 2,
+        out_specs=[pl.BlockSpec(memory_space=pl.ANY)] * 2
+        + [pl.BlockSpec(memory_space=pltpu.VMEM)],
         scratch_shapes=scratch,
         compiler_params=pltpu.CompilerParams(
-            has_side_effects=True, vmem_limit_bytes=58 * 2**20
+            has_side_effects=True, collective_id=0, vmem_limit_bytes=58 * 2**20
         ),
         name="adjoint_cg",
     )(
         cotangent, shear, lame, inertia,
         points[0, 0].transpose(1, 0, 2), counts, maps, pairs[0].transpose(1, 0, 2),
     )
+    on_first, on_second = coef[0, 0], coef[1, 0]
+    displacement = on_first * cotangent - on_second * q1
+    return displacement, cotangent - on_first * q1 + on_second * q2
 
 
 def solution(mesh):

time: 128 us -> 112 us (0.88)
  Pallas kernels: 124 us -> 106 us
  other arithmetic: 0 us -> 4.2 us
  local copies, waits for them, and re-layouts: 3.04 us -> 1.35 us
    pallas_call x1, Pallas kernels: 124 us -> 106 us  [on_device(): pl.pallas_call(functools.partial(kernel, nb, na), out_shape=[jax.ShapeDty...]
    add x0 -> x1, other arithmetic: none -> 4.2 us  [on_device(): return (displacement, cotangent - on_first * q1 + on_second * q2)]
    unnamed x4 -> x2, local copies, waits for them, and re-layouts: 3.04 us -> 0.01 us
    slice x0 -> x1, local copies, waits for them, and re-layouts: none -> 1.35 us  [on_device(): on_first, on_second = (coef[0, 0], coef[1, 0])]
where the time goes in v2:
time: 112 us
  Pallas kernels  106 us (95%)
  other arithmetic  4.2 us (4%)
  local copies, waits for them, and re-layouts  1.35 us (1%)
    pallas_call x1, Pallas kernels, on_device(): pl.pallas_call(functools.partial(kernel, nb, na), out_shape=[jax.ShapeDty...  106 us
    add x1, other arithmetic, on_device(): return (displacement, cotangent - on_first * q1 + on_second * q2)  4.2 us

profile of v2, /device:TPU:1, one launch (start us, length us, event | category | flops | bytes accessed | tf_op | source)
XLA Modules:
  0.0 111.8 jit_solution(16089004192716920912)
XLA Ops:
  0.6 0.0 copy-start
  0.6 105.6 %adjoint_cg.1 = (f32[3,8,32,256]{3,2,1,0:T(8,128)}, f32[3,8,32,256]{3,2,1,0:T(8,128)}, f32[8,128]{1,0:T(8,128)}) custom-call(f32[3,8,32,256]{3,2,1,0:T(8,128)} %c_hbm.1, f32[8,32,256]{2,1,0:T(8,128)} %mu_hbm.1, f32[8,32,256]{2,1,0:T(8,128)} %lam_hbm.1, f32[8,32,256]{2,1,0:T(8,128)} %inertia_hbm.1, f32[3,16,128]{2,1,0:T(8,128)} %bitcast.6, ...), custom_call_target="tpu_custom_call" | custom-call | tf_op jit(solution)/shard_map/adjoint_cg/pallas_call | solution.py:647
  106.2 1.3 %fusion = (f32[1,1]{1,0:T(1,128)}, f32[1,1]{1,0:T(1,128)}) fusion(f32[8,128]{1,0:T(8,128)} %get-tuple-element.5), kind=kLoop, calls=%fused_computation.2 | loop fusion | bytes 16 | tf_op jit(solution)/shard_map/slice | solution.py:669
  107.6 0.0 copy-done
  107.6 4.2 %multiply_add_fusion = (f32[3,8,32,256]{3,2,1,0:T(8,128)}, f32[3,8,32,256]{3,2,1,0:T(8,128)}) fusion(f32[3,8,32,256]{3,2,1,0:T(8,128)} %get-tuple-element.7, f32[3,8,32,256]{3,2,1,0:T(8,128)S(1)} %copy-done, f32[3,8,32,256]{3,2,1,0:T(8,128)} %get-tuple-element.6, f32[]{:T(128)} %bitcast.4, f32[]{:T(128)} %bitcast.3), kind=kLoop, calls=%fused_computation | loop fusion | flops 1376256 | bytes 3932168 | tf_op jit(solution)/shard_map/add | solution.py:671
Async XLA Ops:
  0.6 106.9 %copy-start = (f32[3,8,32,256]{3,2,1,0:T(8,128)S(1)}, f32[3,8,32,256]{3,2,1,0:T(8,128)}, u32[]{:S(2)}) copy-start(f32[3,8,32,256]{3,2,1,0:T(8,128)} %c_hbm.1) | copy-start | bytes 2359300

commit v3 on v2

--- a/solution.py
+++ b/solution.py
@@ -47,9 +47,9 @@
 def kernel(
     nb, na,
     c_hbm, mu_hbm, lam_hbm, inertia_hbm, pts_ref, cnt_ref, map_ref, pair_ref,
-    q1_hbm, q2_hbm, coef_ref,
+    q1_hbm, q2_hbm, first_ref, second_ref,
     cx, qx, q2, mx, inertia, fw, ez, vhm, lhs, ws,
-    moves0, moves1, mparts, pparts, own3, tgtc, ownr, second, rowt, colt, forces,
+    moves0, moves1, mparts, pparts, own3, target3, mines, tgtc, ownr, targetr, second, rowt, colt, forces,
     psend, pgot, msend, mgot, rsend, rgot, fsend, fgot, bsend, bgot,
     ysend, ygot, ysend1, ygot1, arsend, argot,
     sem_in, sem_out, a2a_send, a2a_recv, halo_send, halo_recv, ar_send, ar_recv,
@@ -162,16 +162,23 @@
         )
 
     def send_chunk(phase, src, dst, q):
-        for h in range(4):
-            peer = 4 * q + h
-
-            @pl.when(peer != b)
-            def _():
-                a2a(phase, src, dst, peer).start()
-
-            @pl.when(peer == b)
-            def _():
-                dst[peer] = src[peer]
+        @pl.when(q != me_q)
+        def _():
+            for h in range(4):
+                a2a(phase, src, dst, 4 * q + h).start()
+
+        @pl.when(q == me_q)
+        def _():
+            for h in range(4):
+                peer = 4 * q + h
+
+                @pl.when(peer != b)
+                def _():
+                    a2a(phase, src, dst, peer).start()
+
+                @pl.when(peer == b)
+                def _():
+                    dst[peer] = src[peer]
 
     def wait_chunk(phase, src, dst, q):
         @pl.when(q != me_q)
@@ -340,7 +347,10 @@
     def weigh(g):
         got = eight(pgot, g)
         ids = got[:, MOVE:]
-        ys = tiles(select3(ids, pparts))
+        picked = jnp.where(ids == lane3, 1.0, 0.0).astype(BF16)
+        picked = plain(picked, jnp.concatenate([pparts[...], mparts[...]], axis=1))
+        ys, mine = tiles(picked), picked[:, MOVE:]
+        made = []
         pad = jnp.zeros((WIDTH - 24, WIDTH), F32)
         xs = jnp.concatenate(tiles(got) + [pad], axis=0).T
         for r in range(8):
@@ -351,9 +361,9 @@
             squared = jnp.minimum(squared, 1.0)
             inverse = 1.0 / squared
             weight = 0.005 * (inverse * (inverse + 2.0) - 3.0) - 0.01 * jnp.log(squared)
-            high, low = parts2(weight)
-            ws[g * 8 + r, 0:WIDTH] = high
-            ws[g * 8 + r, WIDTH : 2 * WIDTH] = low
+            made.append(jnp.concatenate(parts2(weight), axis=0))
+            ws[g * 8 + r] = made[r]
+        return made, mine
 
     def halves(value, extra):
         rows = []
@@ -366,11 +376,10 @@
         kept = [jnp.where(keep, row, 0.0) for row in rows]
         return jnp.concatenate(kept, axis=0).astype(BF16)
 
-    def sides(g, dst, mine, first_phase):
+    def sides(g, dst, w, mine, first_phase):
         got = eight(dst, g)
         extra = [ones8, ones8] if first_phase else []
         v_rows, u_rows = halves(got, extra), halves(mine, extra)
-        w = [ws[g * 8 + r] for r in range(8)]
         v_side, w_side = [], []
         for q in range(4):
             kept = only(v_rows, lax.rem(sub8, 4) == q)
@@ -407,12 +416,11 @@
 
     def chunk0(q):
         wait_chunk(0, psend, pgot, q)
-        for g in (2 * q, 2 * q + 1):
-            weigh(g)
         wait_chunk(1, msend, mgot, q)
-        for g in (2 * q, 2 * q + 1):
-            mine = select3(pgot_ids(g), mparts)
-            store_eight(rsend, g, sides(g, mgot, mine, True))
+        weighed = [weigh(g) for g in (2 * q, 2 * q + 1)]
+        made = [sides(2 * q + k, mgot, *weighed[k], True) for k in range(2)]
+        for k in range(2):
+            store_eight(rsend, 2 * q + k, made[k])
         send_chunk(2, rsend, rgot, q)
 
     each_chunk(chunk0, -1)
@@ -429,14 +437,17 @@
             c_c = c_c + cx[c, i + 1] * cx[c, i + 1]
 
 
+    def note_targets():
+        ids = jnp.concatenate([pgot_ids(g) for g in range(groups)], axis=0)
+        target3[...] = jnp.where(ids == lanes3, 1.0, 0.0).astype(BF16)
+        targetr[...] = jnp.sum(jnp.where(eye, ids[:, 0:1], 0.0), axis=0, keepdims=True)
+
     def collect(phase, src, dst):
         batch(phase, src, dst, 0, 0, nb - 1).wait_recv()
         returned = jnp.concatenate([eight(dst, g) for g in range(groups)], axis=0)
-        ids = jnp.concatenate([pgot_ids(g) for g in range(groups)], axis=0)
-        ids_row = jnp.sum(jnp.where(eye, ids[:, 0:1], 0.0), axis=0, keepdims=True)
         block = fiota((BLOCKS, slots), 0)
         to_own = jnp.where(block == ownr[...], 1.0, 0.0).astype(BF16)
-        to_target = jnp.where(block == ids_row, 1.0, 0.0).astype(BF16)
+        to_target = jnp.where(block == targetr[...], 1.0, 0.0).astype(BF16)
         rh, rm = parts2(returned)
         sh, sm = parts2(second[...])
         forces[...] = (plain(to_own, rh) + plain(to_own, rm)) + (
@@ -516,9 +527,11 @@
     def scalar(total, k):
         return jnp.sum(total[k : k + 1], axis=1, keepdims=True)
 
+    note_targets()
     collect(2, rsend, rgot)
     moves1[...] = moves1[...] + forces[...]
     moves_out(3, moves1, fsend, fgot)
+    mines[...] = plain(target3[...], mparts[...])
     spread(qx, 1)
     for c in range(3):
         ysend1[0, c] = qx[c, 1 : ROWS + 1, COLS - 1, :]
@@ -534,9 +547,12 @@
     ar_start(0, 0, rows_of(c_c, c_ec, moves0[...] * forces[...]))
     def chunk1(q):
         wait_chunk(3, fsend, fgot, q)
+        made = []
         for g in (2 * q, 2 * q + 1):
-            mine = select3(pgot_ids(g), mparts)
-            store_eight(bsend, g, sides(g, fgot, mine, False))
+            w = [ws[g * 8 + r] for r in range(8)]
+            made.append(sides(g, fgot, w, mines[rows8(g)], False))
+        for k in range(2):
+            store_eight(bsend, 2 * q + k, made[k])
         send_chunk(4, bsend, bgot, q)
 
     q1_store = pltpu.make_async_copy(qx.at[:, pl.ds(1, ROWS)], q1_hbm, sem_out.at[0])
@@ -580,8 +596,8 @@
     on_first = step0 + step1 * (1.0 + ratio)
     on_second = step1 * step0
 
-    row = iota((8, WIDTH), 0)
-    coef_ref[...] = jnp.where(row == 0, on_first, on_second)
+    first_ref[0] = on_first[0, 0]
+    second_ref[0] = on_second[0, 0]
     for copy in halos0 + halos1:
         copy.wait_send()
 
@@ -591,6 +607,12 @@
         batch(phase, src, dst, 0, 0, nb - 1).wait_send()
     q1_store.wait()
     q2_store.wait()
+
+
+def combine(first_ref, second_ref, c_ref, q1_ref, q2_ref, disp_ref, res_ref):
+    on_first, on_second = first_ref[0], second_ref[0]
+    disp_ref[...] = on_first * c_ref[...] - on_second * q1_ref[...]
+    res_ref[...] = c_ref[...] - on_first * q1_ref[...] + on_second * q2_ref[...]
 
 
 def on_device(nb, na, cotangent, shear, lame, inertia, points, counts, maps, pairs):
@@ -618,7 +640,10 @@
         pltpu.VMEM((WIDTH, MOVE), BF16),
         pltpu.VMEM((WIDTH, MOVE), BF16),
         pltpu.VMEM((slots, WIDTH), BF16),
+        pltpu.VMEM((slots, WIDTH), BF16),
+        pltpu.VMEM((slots, MOVE), F32),
         pltpu.VMEM((slots, WIDTH), F32),
+        pltpu.VMEM((1, slots), F32),
         pltpu.VMEM((1, slots), F32),
         pltpu.VMEM((slots, MOVE), F32),
         pltpu.VMEM((slots, WIDTH), F32),
@@ -644,10 +669,10 @@
         pltpu.SemaphoreType.DMA((2, 2)),
         pltpu.SemaphoreType.DMA((2, 2)),
     ]
-    q1, q2, coef = pl.pallas_call(
+    q1, q2, on_first, on_second = pl.pallas_call(
         functools.partial(kernel, nb, na),
         out_shape=[jax.ShapeDtypeStruct(grid, F32)] * 2
-        + [jax.ShapeDtypeStruct((8, WIDTH), F32)],
+        + [jax.ShapeDtypeStruct((1,), F32)] * 2,
         in_specs=[pl.BlockSpec(memory_space=pl.ANY)] * 4
         + [
             pl.BlockSpec(memory_space=pltpu.VMEM),
@@ -656,7 +681,7 @@
             pl.BlockSpec(memory_space=pltpu.VMEM),
         ],
         out_specs=[pl.BlockSpec(memory_space=pl.ANY)] * 2
-        + [pl.BlockSpec(memory_space=pltpu.VMEM)],
+        + [pl.BlockSpec(memory_space=pltpu.SMEM)] * 2,
         scratch_shapes=scratch,
         compiler_params=pltpu.CompilerParams(
             has_side_effects=True, collective_id=0, vmem_limit_bytes=58 * 2**20
@@ -666,9 +691,16 @@
         cotangent, shear, lame, inertia,
         points[0, 0].transpose(1, 0, 2), counts, maps, pairs[0].transpose(1, 0, 2),
     )
-    on_first, on_second = coef[0, 0], coef[1, 0]
-    displacement = on_first * cotangent - on_second * q1
-    return displacement, cotangent - on_first * q1 + on_second * q2
+    part = pl.BlockSpec((3, 2, COLS, DEPTH), lambda i: (0, i, 0, 0))
+    number = pl.BlockSpec(memory_space=pltpu.SMEM)
+    return pl.pallas_call(
+        combine,
+        grid=(ROWS // 2,),
+        out_shape=[jax.ShapeDtypeStruct(grid, F32)] * 2,
+        in_specs=[number, number, part, part, part],
+        out_specs=[part, part],
+        name="combine",
+    )(on_first, on_second, cotangent, q1, q2)
 
 
 def solution(mesh):

time: 112 us -> 106 us (0.946)
  other arithmetic: 4.2 us -> 0 us
  local copies, waits for them, and re-layouts: 1.35 us -> 0 us
    pallas_call x1, Pallas kernels: 106 us -> 99.7 us  [on_device(): pl.pallas_call(functools.partial(kernel, nb, na), out_shape=[jax.ShapeDty...]
    pallas_call x0 -> x1, Pallas kernels: none -> 5.1 us  [on_device(): pl.pallas_call(combine, grid=(ROWS // 2,), out_shape=[jax.ShapeDtypeStruc...]
    add x1 -> x0, other arithmetic: 4.2 us -> none  [on_device(): return (displacement, cotangent - on_first * q1 + on_second * q2)]
    slice x1 -> x0, local copies, waits for them, and re-layouts: 1.35 us -> none  [on_device(): on_first, on_second = (coef[0, 0], coef[1, 0])]
where the time goes in v3:
time: 106 us; the launch traced here: 105 us
  Pallas kernels  105 us (99%)
    pallas_call x1, Pallas kernels, on_device(): pl.pallas_call(functools.partial(kernel, nb, na), out_shape=[jax.ShapeDty...  99.7 us
    pallas_call x1, Pallas kernels, on_device(): pl.pallas_call(combine, grid=(ROWS // 2,), out_shape=[jax.ShapeDtypeStruc...  5.1 us

profile of v3, /device:TPU:1, one launch (start us, length us, event | category | flops | bytes accessed | tf_op | source)
XLA Modules:
  0.0 105.5 jit_solution(9131290122263597117)
XLA Ops:
  0.6 99.7 %adjoint_cg.1 = (f32[3,8,32,256]{3,2,1,0:T(8,128)}, f32[3,8,32,256]{3,2,1,0:T(8,128)}, f32[1]{0:T(128)}, f32[1]{0:T(128)}) custom-call(f32[3,8,32,256]{3,2,1,0:T(8,128)} %c_ref.1, f32[8,32,256]{2,1,0:T(8,128)} %mu_hbm.1, f32[8,32,256]{2,1,0:T(8,128)} %lam_hbm.1, f32[8,32,256]{2,1,0:T(8,128)} %inertia_hbm.1, f32[3,16,128]{2,1,0:T(8,128)} %bitcast.4, ...), custom_call_target="tpu_custom_call" | custom-call | tf_op jit(solution)/shard_map/adjoint_cg/pallas_call | solution.py:672
  100.4 5.1 %combine.1 = (f32[3,8,32,256]{3,2,1,0:T(8,128)}, f32[3,8,32,256]{3,2,1,0:T(8,128)}) custom-call(f32[1]{0:T(128)} %get-tuple-element.6.first_ref, f32[1]{0:T(128)} %get-tuple-element.7.second_ref, f32[3,8,32,256]{3,2,1,0:T(8,128)} %c_ref.1, f32[3,8,32,256]{3,2,1,0:T(8,128)} %get-tuple-element.8.q1_ref, f32[3,8,32,256]{3,2,1,0:T(8,128)} %get-tuple-element.9.q2_ref), custom_call_target="tpu_custom_call" | custom-call | tf_op jit(solution)/shard_map/combine/pallas_call | solution.py:696

commit v4 on v3

--- a/solution.py
+++ b/solution.py
@@ -47,12 +47,12 @@
 def kernel(
     nb, na,
     c_hbm, mu_hbm, lam_hbm, inertia_hbm, pts_ref, cnt_ref, map_ref, pair_ref,
-    q1_hbm, q2_hbm, first_ref, second_ref,
+    disp_ref, res_ref,
     cx, qx, q2, mx, inertia, fw, ez, vhm, lhs, ws,
     moves0, moves1, mparts, pparts, own3, target3, mines, tgtc, ownr, targetr, second, rowt, colt, forces,
-    psend, pgot, msend, mgot, rsend, rgot, fsend, fgot, bsend, bgot,
+    psend, pgot, rsend, rgot, fsend, fgot, bsend, bgot,
     ysend, ygot, ysend1, ygot1, arsend, argot,
-    sem_in, sem_out, a2a_send, a2a_recv, halo_send, halo_recv, ar_send, ar_recv,
+    sem_in, a2a_send, a2a_recv, halo_send, halo_recv, ar_send, ar_recv,
 ):
     b = lax.axis_index("body")
     a = lax.axis_index("across")
@@ -200,7 +200,6 @@
         for k in range(nb):
             ref[k] = value[k * CAP : (k + 1) * CAP]
 
-    store_all(psend, jnp.concatenate([plain(own3[...], pparts[...]), tgtc[...]], axis=1))
     def map_row(k):
         pair = map_ref[0, 0, pl.ds(2 * k, 1), :], map_ref[0, 0, pl.ds(2 * k + 1, 1), :]
         return jnp.concatenate(pair, axis=1)
@@ -212,10 +211,43 @@
 
     lax.fori_loop(0, BLOCKS // 2, place, 0)
 
-    pl.semaphore_wait(barrier, nb - 1 + (na - 1) * (nb // near))
-    each_chunk(lambda q: send_chunk(0, psend, pgot, q), 1)
+    def pick(vector, base, moves):
+        for c in range(3):
+            flat = vector[c, base : base + ROWS].reshape(ROWS * COLS, DEPTH)
+            at = slice(c * 256, (c + 1) * 256)
+            vhm[at, :DEPTH], vhm[at, DEPTH:] = parts2(flat)
+
+        def step(k, rows):
+            picked = plain(vhm[...], jnp.concatenate([ez[k], ez[k]], axis=0))
+            mask = iota((256, 2 * WIDTH), 0) == map_row(k) // DEPTH
+            made = []
+            for c in range(3):
+                kept = jnp.where(mask, picked[c * 256 : (c + 1) * 256], 0.0)
+                row = jnp.sum(kept, axis=0, keepdims=True)
+                lower = jnp.where(block_id == 2 * k, row[:, :WIDTH], rows[c])
+                made.append(jnp.where(block_id == 2 * k + 1, row[:, WIDTH:], lower))
+            return tuple(made)
+
+        rows = lax.fori_loop(0, BLOCKS // 2, step, (pad16,) * 3)
+        moves[...] = jnp.concatenate(rows, axis=1)
+
     for load in loads:
         load.wait()
+    pick(cx, 1, moves0)
+
+    def tiles(value):
+        return [value[:, c * WIDTH : (c + 1) * WIDTH] for c in range(3)]
+
+    def moves_out(phase, moves, src, dst):
+        store_parts(mparts, tiles(moves[...]))
+
+        store_all(src, plain(own3[...], mparts[...]))
+        each_chunk(lambda q: send_chunk(phase, src, dst, q), 1)
+
+    store_parts(mparts, tiles(moves0[...]))
+    first = [plain(own3[...], pparts[...]), tgtc[...], plain(own3[...], mparts[...])]
+    store_all(psend, jnp.concatenate(first, axis=1))
+
     up, down = wrap(b + 1, nb), wrap(b - 1, nb)
     right, left = wrap(a + 1, na), wrap(a - 1, na)
 
@@ -240,41 +272,10 @@
         halo(4, ysend.at[0], ygot.at[0], (b, right)),
         halo(5, ysend.at[1], ygot.at[1], (b, left)),
     ]
+    pl.semaphore_wait(barrier, nb - 1 + (na - 1) * (nb // near))
+    each_chunk(lambda q: send_chunk(0, psend, pgot, q), 1)
     for copy in halos0:
         copy.start()
-
-    def pick(vector, base, moves):
-        for c in range(3):
-            flat = vector[c, base : base + ROWS].reshape(ROWS * COLS, DEPTH)
-            at = slice(c * 256, (c + 1) * 256)
-            vhm[at, :DEPTH], vhm[at, DEPTH:] = parts2(flat)
-
-        def step(k, rows):
-            picked = plain(vhm[...], jnp.concatenate([ez[k], ez[k]], axis=0))
-            mask = iota((256, 2 * WIDTH), 0) == map_row(k) // DEPTH
-            made = []
-            for c in range(3):
-                kept = jnp.where(mask, picked[c * 256 : (c + 1) * 256], 0.0)
-                row = jnp.sum(kept, axis=0, keepdims=True)
-                lower = jnp.where(block_id == 2 * k, row[:, :WIDTH], rows[c])
-                made.append(jnp.where(block_id == 2 * k + 1, row[:, WIDTH:], lower))
-            return tuple(made)
-
-        rows = lax.fori_loop(0, BLOCKS // 2, step, (pad16,) * 3)
-        moves[...] = jnp.concatenate(rows, axis=1)
-
-    pick(cx, 1, moves0)
-
-    def tiles(value):
-        return [value[:, c * WIDTH : (c + 1) * WIDTH] for c in range(3)]
-
-    def moves_out(phase, moves, src, dst):
-        store_parts(mparts, tiles(moves[...]))
-
-        store_all(src, plain(own3[...], mparts[...]))
-        each_chunk(lambda q: send_chunk(phase, src, dst, q), 1)
-
-    moves_out(1, moves0, msend, mgot)
 
     row32, lane256 = iota((COLS, DEPTH), 0), iota((COLS, DEPTH), 1)
 
@@ -346,7 +347,7 @@
 
     def weigh(g):
         got = eight(pgot, g)
-        ids = got[:, MOVE:]
+        ids = got[:, MOVE : MOVE + WIDTH]
         picked = jnp.where(ids == lane3, 1.0, 0.0).astype(BF16)
         picked = plain(picked, jnp.concatenate([pparts[...], mparts[...]], axis=1))
         ys, mine = tiles(picked), picked[:, MOVE:]
@@ -363,7 +364,7 @@
             weight = 0.005 * (inverse * (inverse + 2.0) - 3.0) - 0.01 * jnp.log(squared)
             made.append(jnp.concatenate(parts2(weight), axis=0))
             ws[g * 8 + r] = made[r]
-        return made, mine
+        return got[:, MOVE + WIDTH :], made, mine
 
     def halves(value, extra):
         rows = []
@@ -376,8 +377,7 @@
         kept = [jnp.where(keep, row, 0.0) for row in rows]
         return jnp.concatenate(kept, axis=0).astype(BF16)
 
-    def sides(g, dst, w, mine, first_phase):
-        got = eight(dst, g)
+    def sides(g, got, w, mine, first_phase):
         extra = [ones8, ones8] if first_phase else []
         v_rows, u_rows = halves(got, extra), halves(mine, extra)
         v_side, w_side = [], []
@@ -412,13 +412,12 @@
         )
 
     def pgot_ids(g):
-        return jnp.concatenate([pgot[2 * g, :, MOVE:], pgot[2 * g + 1, :, MOVE:]], axis=0)
+        return jnp.concatenate([pgot[2 * g, :, MOVE : MOVE + WIDTH], pgot[2 * g + 1, :, MOVE : MOVE + WIDTH]], axis=0)
 
     def chunk0(q):
         wait_chunk(0, psend, pgot, q)
-        wait_chunk(1, msend, mgot, q)
         weighed = [weigh(g) for g in (2 * q, 2 * q + 1)]
-        made = [sides(2 * q + k, mgot, *weighed[k], True) for k in range(2)]
+        made = [sides(2 * q + k, *weighed[k], True) for k in range(2)]
         for k in range(2):
             store_eight(rsend, 2 * q + k, made[k])
         send_chunk(2, rsend, rgot, q)
@@ -550,13 +549,11 @@
         made = []
         for g in (2 * q, 2 * q + 1):
             w = [ws[g * 8 + r] for r in range(8)]
-            made.append(sides(g, fgot, w, mines[rows8(g)], False))
+            made.append(sides(g, eight(fgot, g), w, mines[rows8(g)], False))
         for k in range(2):
             store_eight(bsend, 2 * q + k, made[k])
         send_chunk(4, bsend, bgot, q)
 
-    q1_store = pltpu.make_async_copy(qx.at[:, pl.ds(1, ROWS)], q1_hbm, sem_out.at[0])
-    q1_store.start()
     each_chunk(chunk1, -1, 0, chunks // 2)
     ar_start(0, 1, ar_finish(0, 0))
     each_chunk(chunk1, -1, chunks // 2, chunks)
@@ -585,8 +582,6 @@
     r_moves = moves0[...] - step0 * moves1[...]
     ar_start(1, 0, rows_of(r_r, r_ar, -step0 * (r_moves * forces[...])))
     spread(q2, 0)
-    q2_store = pltpu.make_async_copy(q2, q2_hbm, sem_out.at[1])
-    q2_store.start()
     ar_start(1, 1, ar_finish(1, 0))
     total1 = ar_finish(1, 1)
     norm1 = scalar(total1, 0)
@@ -596,23 +591,22 @@
     on_first = step0 + step1 * (1.0 + ratio)
     on_second = step1 * step0
 
-    first_ref[0] = on_first[0, 0]
-    second_ref[0] = on_second[0, 0]
+
+    def finish(i, carry):
+        for c in range(3):
+            v, q = cx[c, i + 1], qx[c, i + 1]
+            disp_ref[c, i] = on_first * v - on_second * q
+            res_ref[c, i] = v - on_first * q + on_second * q2[c, i]
+        return carry
+
+    lax.fori_loop(0, ROWS, finish, 0)
     for copy in halos0 + halos1:
         copy.wait_send()
 
-    for phase, (src, dst) in enumerate(
-        ((psend, pgot), (msend, mgot), (rsend, rgot), (fsend, fgot), (bsend, bgot))
+    for phase, src, dst in (
+        (0, psend, pgot), (2, rsend, rgot), (3, fsend, fgot), (4, bsend, bgot)
     ):
         batch(phase, src, dst, 0, 0, nb - 1).wait_send()
-    q1_store.wait()
-    q2_store.wait()
-
-
-def combine(first_ref, second_ref, c_ref, q1_ref, q2_ref, disp_ref, res_ref):
-    on_first, on_second = first_ref[0], second_ref[0]
-    disp_ref[...] = on_first * c_ref[...] - on_second * q1_ref[...]
-    res_ref[...] = c_ref[...] - on_first * q1_ref[...] + on_second * q2_ref[...]
 
 
 def on_device(nb, na, cotangent, shear, lame, inertia, points, counts, maps, pairs):
@@ -649,8 +643,7 @@
         pltpu.VMEM((slots, WIDTH), F32),
         pltpu.VMEM((slots, WIDTH), F32),
         pltpu.VMEM((BLOCKS, MOVE), F32),
-        *buffers(MOVE + WIDTH),
-        *buffers(MOVE),
+        *buffers(MOVE + WIDTH + MOVE),
         *buffers(MOVE),
         *buffers(MOVE),
         *buffers(MOVE),
@@ -661,7 +654,6 @@
         pltpu.VMEM((2, 2, 8, WIDTH), F32),
         pltpu.VMEM((2, 2, peers, 8, WIDTH), F32),
         pltpu.SemaphoreType.DMA((4,)),
-        pltpu.SemaphoreType.DMA((2,)),
         pltpu.SemaphoreType.DMA((5,)),
         pltpu.SemaphoreType.DMA((5, nb // 4)),
         pltpu.SemaphoreType.DMA((10,)),
@@ -669,10 +661,9 @@
         pltpu.SemaphoreType.DMA((2, 2)),
         pltpu.SemaphoreType.DMA((2, 2)),
     ]
-    q1, q2, on_first, on_second = pl.pallas_call(
+    return pl.pallas_call(
         functools.partial(kernel, nb, na),
-        out_shape=[jax.ShapeDtypeStruct(grid, F32)] * 2
-        + [jax.ShapeDtypeStruct((1,), F32)] * 2,
+        out_shape=[pltpu.VMEM(grid, F32)] * 2,
         in_specs=[pl.BlockSpec(memory_space=pl.ANY)] * 4
         + [
             pl.BlockSpec(memory_space=pltpu.VMEM),
@@ -680,27 +671,16 @@
             pl.BlockSpec(memory_space=pltpu.VMEM),
             pl.BlockSpec(memory_space=pltpu.VMEM),
         ],
-        out_specs=[pl.BlockSpec(memory_space=pl.ANY)] * 2
-        + [pl.BlockSpec(memory_space=pltpu.SMEM)] * 2,
+        out_specs=[pl.BlockSpec(memory_space=pltpu.VMEM)] * 2,
         scratch_shapes=scratch,
         compiler_params=pltpu.CompilerParams(
-            has_side_effects=True, collective_id=0, vmem_limit_bytes=58 * 2**20
+            has_side_effects=True, collective_id=0, vmem_limit_bytes=54 * 2**20
         ),
         name="adjoint_cg",
     )(
         cotangent, shear, lame, inertia,
         points[0, 0].transpose(1, 0, 2), counts, maps, pairs[0].transpose(1, 0, 2),
     )
-    part = pl.BlockSpec((3, 2, COLS, DEPTH), lambda i: (0, i, 0, 0))
-    number = pl.BlockSpec(memory_space=pltpu.SMEM)
-    return pl.pallas_call(
-        combine,
-        grid=(ROWS // 2,),
-        out_shape=[jax.ShapeDtypeStruct(grid, F32)] * 2,
-        in_specs=[number, number, part, part, part],
-        out_specs=[part, part],
-        name="combine",
-    )(on_first, on_second, cotangent, q1, q2)
 
 
 def solution(mesh):

time: 106 us -> 91.2 us (0.86)
  Pallas kernels: 105 us -> 88.7 us
  local copies, waits for them, and re-layouts: 0 us -> 1.76 us
    pallas_call x2 -> x1, Pallas kernels: 105 us -> 88.7 us  [on_device(): pl.pallas_call(functools.partial(kernel, nb, na), out_shape=[pltpu.VMEM(g...]
    unnamed x0 -> x2, local copies, waits for them, and re-layouts: none -> 1.76 us
where the time goes in v4:
time: 91.2 us; the launch traced here: 91.1 us
  Pallas kernels  88.7 us (97%)
  local copies, waits for them, and re-layouts  1.76 us (2%)
    pallas_call x1, Pallas kernels, on_device(): pl.pallas_call(functools.partial(kernel, nb, na), out_shape=[pltpu.VMEM(g...  88.7 us

profile of v4, /device:TPU:1, one launch (start us, length us, event | category | flops | bytes accessed | tf_op | source)
XLA Modules:
  0.0 91.1 jit_solution(15951341231456818059)
XLA Ops:
  0.6 88.7 %adjoint_cg.1 = (f32[3,8,32,256]{3,2,1,0:T(8,128)S(1)}, f32[3,8,32,256]{3,2,1,0:T(8,128)S(1)}) custom-call(f32[3,8,32,256]{3,2,1,0:T(8,128)} %c_hbm.1, f32[8,32,256]{2,1,0:T(8,128)} %mu_hbm.1, f32[8,32,256]{2,1,0:T(8,128)} %lam_hbm.1, f32[8,32,256]{2,1,0:T(8,128)} %inertia_hbm.1, f32[3,16,128]{2,1,0:T(8,128)} %bitcast.4, s32[1,1,16]{2,1,0:T(1,128)} %cnt_ref.1, ...), custom_call_target="tpu_custom_call" | custom-call | tf_op jit(solution)/shard_map/adjoint_cg/pallas_call | solution.py:664
  89.3 0.9 copy.12
  90.2 0.9 copy.13

commit v5 on v4

--- a/solution.py
+++ b/solution.py
@@ -49,7 +49,7 @@
     c_hbm, mu_hbm, lam_hbm, inertia_hbm, pts_ref, cnt_ref, map_ref, pair_ref,
     disp_ref, res_ref,
     cx, qx, q2, mx, inertia, fw, ez, vhm, lhs, ws,
-    moves0, moves1, mparts, pparts, own3, target3, mines, tgtc, ownr, targetr, second, rowt, colt, forces,
+    moves0, moves1, mparts, pparts, own3, target3, mines0, mines, tgtc, ownr, targetr, second, rowt, colt, forces,
     psend, pgot, rsend, rgot, fsend, fgot, bsend, bgot,
     ysend, ygot, ysend1, ygot1, arsend, argot,
     sem_in, a2a_send, a2a_recv, halo_send, halo_recv, ar_send, ar_recv,
@@ -189,12 +189,12 @@
         def _():
             batch(phase, src, dst, q, 4 * q, 3).wait_recv()
 
-    def each_chunk(body, sign, start=0, stop=nb // 4):
+    def each_chunk(body, sign):
         def step(t, carry):
             body(wrap(me_q + sign * t, chunks))
             return carry
 
-        lax.fori_loop(start, stop, step, 0)
+        lax.fori_loop(0, chunks, step, 0)
 
     def store_all(ref, value):
         for k in range(nb):
@@ -404,12 +404,14 @@
         def force(move, total, parts, c):
             return move * total - (parts[2 * c] + parts[2 * c + 1])
 
-        second[at] = jnp.concatenate(
+        to_keep = jnp.concatenate(
             [force(u, col_total, into_second, c) for c, u in enumerate(tiles(mine))], axis=1
         )
-        return jnp.concatenate(
+        second[at] = to_keep
+        to_return = jnp.concatenate(
             [force(v, row_total, into_first, c) for c, v in enumerate(tiles(got))], axis=1
         )
+        return to_return, to_keep
 
     def pgot_ids(g):
         return jnp.concatenate([pgot[2 * g, :, MOVE : MOVE + WIDTH], pgot[2 * g + 1, :, MOVE : MOVE + WIDTH]], axis=0)
@@ -419,9 +421,15 @@
         weighed = [weigh(g) for g in (2 * q, 2 * q + 1)]
         made = [sides(2 * q + k, *weighed[k], True) for k in range(2)]
         for k in range(2):
-            store_eight(rsend, 2 * q + k, made[k])
+            store_eight(rsend, 2 * q + k, made[k][0])
+            mines0[rows8(2 * q + k)] = weighed[k][2]
         send_chunk(2, rsend, rgot, q)
 
+    c_c = jnp.zeros((1, DEPTH), F32)
+    for c in range(3):
+        for i in range(ROWS):
+            square = cx[c, i + 1] * cx[c, i + 1]
+            c_c = c_c + jnp.sum(square, axis=0, keepdims=True)
     each_chunk(chunk0, -1)
 
     for copy in halos0:
@@ -430,10 +438,6 @@
     lax.fori_loop(0, ROWS, faces, 0)
     (c_ec,) = elastic(cx, ygot, qx, 1, (cx,))
     pick(qx, 1, moves1)
-    c_c = jnp.zeros((COLS, DEPTH), F32)
-    for c in range(3):
-        for i in range(ROWS):
-            c_c = c_c + cx[c, i + 1] * cx[c, i + 1]
 
 
     def note_targets():
@@ -544,19 +548,36 @@
     for copy in halos1:
         copy.start()
     ar_start(0, 0, rows_of(c_c, c_ec, moves0[...] * forces[...]))
-    def chunk1(q):
-        wait_chunk(3, fsend, fgot, q)
+    together = 2 if chunks % 4 == 0 else 1
+
+    def fold(value):
+        return sum(tiles(value))
+
+    def chunks1(t, sums):
+        with_c, with_q = sums
+        here = [wrap(me_q - together * t - k, chunks) for k in range(together)]
+        for q in here:
+            wait_chunk(3, fsend, fgot, q)
         made = []
-        for g in (2 * q, 2 * q + 1):
+        for g in [2 * q + k for q in here for k in range(2)]:
             w = [ws[g * 8 + r] for r in range(8)]
-            made.append(sides(g, eight(fgot, g), w, mines[rows8(g)], False))
-        for k in range(2):
-            store_eight(bsend, 2 * q + k, made[k])
-        send_chunk(4, bsend, bgot, q)
-
-    each_chunk(chunk1, -1, 0, chunks // 2)
+            got, mine = eight(fgot, g), mines[rows8(g)]
+            to_return, to_keep = sides(g, got, w, mine, False)
+            got0, mine0 = eight(pgot, g)[:, MOVE + WIDTH :], mines0[rows8(g)]
+            with_c = with_c + fold(got0 * to_return + mine0 * to_keep)
+            with_q = with_q + fold(got * to_return + mine * to_keep)
+            made.append((g, to_return))
+        for g, value in made:
+            store_eight(bsend, g, value)
+        for q in here:
+            send_chunk(4, bsend, bgot, q)
+        return with_c, with_q
+
+    steps = chunks // together
+    sums = (jnp.zeros((8, WIDTH), F32),) * 2
+    sums = lax.fori_loop(0, steps // 2, chunks1, sums)
     ar_start(0, 1, ar_finish(0, 0))
-    each_chunk(chunk1, -1, chunks // 2, chunks)
+    contact_c, contact_q = lax.fori_loop(steps // 2, steps, chunks1, sums)
     for copy in halos1:
         copy.wait_recv()
     clear_edges((qx,), ygot1)
@@ -578,11 +599,10 @@
 
     zero = jnp.zeros((COLS, DEPTH), F32)
     r_r, r_ar = lax.fori_loop(0, ROWS, products, (zero, zero))
+    ar_start(1, 0, rows_of(r_r, r_ar, -step0 * (contact_c - step0 * contact_q)))
     collect(4, bsend, bgot)
-    r_moves = moves0[...] - step0 * moves1[...]
-    ar_start(1, 0, rows_of(r_r, r_ar, -step0 * (r_moves * forces[...])))
+    ar_start(1, 1, ar_finish(1, 0))
     spread(q2, 0)
-    ar_start(1, 1, ar_finish(1, 0))
     total1 = ar_finish(1, 1)
     norm1 = scalar(total1, 0)
     product = scalar(total1, 1) + scalar(total1, 2)
@@ -635,6 +655,7 @@
         pltpu.VMEM((WIDTH, MOVE), BF16),
         pltpu.VMEM((slots, WIDTH), BF16),
         pltpu.VMEM((slots, WIDTH), BF16),
+        pltpu.VMEM((slots, MOVE), F32),
         pltpu.VMEM((slots, MOVE), F32),
         pltpu.VMEM((slots, WIDTH), F32),
         pltpu.VMEM((1, slots), F32),

time: 91.2 us -> 89.3 us (0.979)
  Pallas kernels: 88.7 us -> 86.7 us
    pallas_call x1, Pallas kernels: 88.7 us -> 86.7 us  [on_device(): pl.pallas_call(functools.partial(kernel, nb, na), out_shape=[pltpu.VMEM(g...]
where the time goes in v5:
time: 89.3 us; the launch traced here: 89.1 us
  Pallas kernels  86.7 us (97%)
  local copies, waits for them, and re-layouts  1.76 us (2%)
    pallas_call x1, Pallas kernels, on_device(): pl.pallas_call(functools.partial(kernel, nb, na), out_shape=[pltpu.VMEM(g...  86.7 us

profile of v5, /device:TPU:1, one launch (start us, length us, event | category | flops | bytes accessed | tf_op | source)
XLA Modules:
  0.0 89.1 jit_solution(7847330540762362333)
XLA Ops:
  0.6 86.7 %adjoint_cg.1 = (f32[3,8,32,256]{3,2,1,0:T(8,128)S(1)}, f32[3,8,32,256]{3,2,1,0:T(8,128)S(1)}) custom-call(f32[3,8,32,256]{3,2,1,0:T(8,128)} %c_hbm.1, f32[8,32,256]{2,1,0:T(8,128)} %mu_hbm.1, f32[8,32,256]{2,1,0:T(8,128)} %lam_hbm.1, f32[8,32,256]{2,1,0:T(8,128)} %inertia_hbm.1, f32[3,16,128]{2,1,0:T(8,128)} %bitcast.4, s32[1,1,16]{2,1,0:T(1,128)} %cnt_ref.1, ...), custom_call_target="tpu_custom_call" | custom-call | tf_op jit(solution)/shard_map/adjoint_cg/pallas_call | solution.py:685
  87.4 0.9 copy.12
  88.2 0.9 copy.13
